TPU v7x, 256 devices: a whole 4x4x8 slice. The times are simulated.
256 devices in a mesh: list: 32 (over z_lo, y, core), tensor: 8 (over x, z_hi).
Axes of the slice: x: 4, y: 4, z: 8 (z_hi: 2, z_lo: 4; z = z_hi * 4 + z_lo), core: 2. Of those that a mesh axis runs over, the one named last changes fastest.
Arguments:
- states: bfloat16 [768, 16, 4096], P('list', None, 'tensor')
- lengths: int32 [768], P('list'), may hold values from 2 to 16, as said below
- assign: int32 [768], P('list'), may hold values from 0 to 131071, as said below
- norm_gain: float32 [4096], replicated, may hold values from 0.1 to 1.9
- gate_weight: bfloat16 [4096, 7168], P('list', 'tensor'), may hold values from -0.09375 to 0.09375
- up_weight: bfloat16 [4096, 7168], P('list', 'tensor'), may hold values from -0.09375 to 0.09375
- down_weight: bfloat16 [7168, 4096], P('tensor', 'list'), may hold values from -0.0625 to 0.0625
- out_gain: float32 [4096], P('tensor'), may hold values from 0.25 to 1.75
- centroids: bfloat16 [131072, 4096], P('list', 'tensor'), may hold values from -6 to 6
Outputs:
- embedding: float32 [768, 4096], P('list', 'tensor')
- residual: float32 [768, 4096], P('list', 'tensor')
Inputs may be any that keep to these rules, and one draw needn't show every extreme that they name: `lengths`: some passage has all 16 slots filled in every draw. `assign`: centroids of index o of list are rows o * 4096 to (o + 1) * 4096 - 1. Of the 24 passages of one index of list at most 2 are assigned to centroids of any one index of list, and in every draw some index of list is assigned exactly 2 passages by every index of list.
All inputs are finite; a program needn't handle non-finite values.
Results may differ from a plain program's by a relative error of at most 0.0065.
Values may be sent and summed in bfloat16 or wider, within the bound.
A program may use at most 128 MiB of HBM per device.

v0:
```python
import jax
import jax.numpy as jnp
from jax import lax
from jax.sharding import PartitionSpec as P

CAP = 2


def per_device(
    states, lengths, assign, norm_gain, gate_weight, up_weight, down_weight, out_gain, centroids
):
    passes, seq, width_part = states.shape
    whole = lax.all_gather(states, "tensor", axis=2, tiled=True)
    width = whole.shape[2]
    rows_n = passes * seq
    flat = whole.reshape(rows_n, width).astype(jnp.float32)
    scale = lax.rsqrt(jnp.mean(flat * flat, axis=1, keepdims=True) + 1e-05)
    normed = (flat * scale * norm_gain[None, :]).astype(jnp.bfloat16)
    gate = jnp.dot(
        normed,
        lax.all_gather(gate_weight, "list", axis=0, tiled=True),
        preferred_element_type=jnp.float32,
    )
    up = jnp.dot(
        normed,
        lax.all_gather(up_weight, "list", axis=0, tiled=True),
        preferred_element_type=jnp.float32,
    )
    hidden = (jax.nn.silu(gate) * up).astype(jnp.bfloat16)
    slots = jnp.arange(seq, dtype=jnp.int32)
    valid = (slots[None, :] < lengths[:, None]).astype(jnp.float32)
    pool_w = valid / lengths[:, None].astype(jnp.float32)
    own_states = states.astype(jnp.float32)
    terms = jnp.dot(
        hidden,
        lax.all_gather(down_weight, "list", axis=1, tiled=True),
        preferred_element_type=jnp.float32,
    )
    mixed = lax.psum_scatter(terms, "tensor", scatter_dimension=1, tiled=True)
    layer = own_states + mixed.reshape(passes, seq, width_part)
    pooled = jnp.einsum("ps,psd->pd", pool_w, layer)
    total = lax.psum(jnp.sum(pooled * pooled, axis=1), "tensor")
    embedding = pooled * lax.rsqrt(total[:, None] / width + 1e-05) * out_gain[None, :]
    n_list = lax.axis_size("list")
    per_owner = centroids.shape[0]
    owner = assign // per_owner
    local_id = assign - owner * per_owner
    places = jnp.arange(passes, dtype=jnp.int32)
    same_owner = owner[:, None] == owner[None, :]
    earlier = places[:, None] > places[None, :]
    rank = jnp.sum((same_owner & earlier).astype(jnp.int32), axis=1)
    owner_hit = owner[None, None, :] == jnp.arange(n_list, dtype=jnp.int32)[:, None, None]
    slot_hit = rank[None, None, :] == jnp.arange(CAP, dtype=jnp.int32)[None, :, None]
    select_int = (owner_hit & slot_hit).astype(jnp.int32)
    select = select_int.astype(jnp.float32)
    send_id = jnp.sum(select_int * local_id[None, None, :], axis=2)
    send_rows = jnp.einsum("ocp,pd->ocd", select, embedding, precision=lax.Precision.HIGHEST)
    got_rows = lax.all_to_all(send_rows, "list", split_axis=0, concat_axis=0, tiled=True)
    got_id = lax.all_to_all(send_id, "list", split_axis=0, concat_axis=0, tiled=True)
    differences = got_rows - jnp.take(centroids, got_id, axis=0).astype(jnp.float32)
    returned = lax.all_to_all(differences, "list", split_axis=0, concat_axis=0, tiled=True)
    residual = jnp.einsum("ocp,ocd->pd", select, returned, precision=lax.Precision.HIGHEST)
    return (embedding, residual)


def solution(mesh):
    return jax.shard_map(
        per_device,
        mesh=mesh,
        in_specs=(
            P("list", None, "tensor"),
            P("list"),
            P("list"),
            P(),
            P("list", "tensor"),
            P("list", "tensor"),
            P("tensor", "list"),
            P("tensor"),
            P("list", "tensor"),
        ),
        out_specs=(P("list", "tensor"), P("list", "tensor")),
        check_vma=False,
    )
```

profile of v0, /device:TPU:6, one launch (start us, length us, event | category | flops | bytes accessed | tf_op | source)
XLA Modules:
  0.0 554.6 jit_solution(4250680985617438824)
XLA Ops:
  7.2 0.0 copy-start.4
  7.2 0.0 all-gather.5.cloned.1.call-start
  7.2 0.7 all-gather.5.cloned.1.call-update
  7.9 0.0 all-gather.7.cloned.1.call-start
  8.0 0.7 all-gather.7.cloned.1.call-update
  8.7 0.0 all-gather.11.cloned.1.call-start
  8.7 0.7 all-gather.11.cloned.1.call-update
  9.4 0.0 all-gather.9.cloned.1.call-start
  9.4 0.5 all-gather.9.cloned.1.call-update
  10.0 0.0 reduce-scatter.2.cloned.1.call-start
  10.0 96.9 %all-gather.5.cloned.1.call-done = bf16[24,16,4096]{2,1,0:T(8,128)(2,1)} async-done(((bf16[24,16,512]{2,1,0:T(8,128)(2,1)}), bf16[24,16,4096]{2,1,0:T(8,128)(2,1)}) %all-gather.5.cloned.1.call-update) | async-done | bytes 3145744 | tf_op jit(solution)/shard_map/all_gather | solution.py:13
  106.9 0.0 copy-start
  106.9 2.7 multiply_reduce_fusion
  109.7 0.1 rsqrt.16
  109.8 0.0 copy-done.4
  109.8 0.0 copy-done
  109.8 2.7 fusion.1
  112.5 0.0 copy-start.1
  112.5 60.5 %all-gather.7.cloned.1.call-done = bf16[4096,896]{1,0:T(8,128)(2,1)} async-done(((bf16[128,896]{1,0:T(8,128)(2,1)}), bf16[4096,896]{1,0:T(8,128)(2,1)}) %all-gather.7.cloned.1.call-update) | async-done | bytes 7340048 | tf_op jit(solution)/shard_map/all_gather | solution.py:21
  173.0 8.6 %fusion.22 = f32[384,896]{1,0:T(8,128)} fusion(bf16[384,4096]{1,0:T(8,128)(2,1)} %fusion.1, bf16[4096,896]{1,0:T(8,128)(2,1)} %all-gather.7.cloned.1.call-done), kind=kOutput, calls=%fused_computation.48 | convolution fusion | flops 2818572288 | bytes 11862016 | tf_op jit(solution)/shard_map/dot_general | solution.py:19
  181.7 74.8 %all-gather.11.cloned.1.call-done = bf16[896,4096]{1,0:T(8,128)(2,1)} async-done(((bf16[896,128]{1,0:T(8,128)(2,1)}), bf16[896,4096]{1,0:T(8,128)(2,1)}) %all-gather.11.cloned.1.call-update) | async-done | bytes 7340048 | tf_op jit(solution)/shard_map/all_gather | solution.py:36
  256.4 68.9 %all-gather.9.cloned.1.call-done = bf16[4096,896]{1,0:T(8,128)(2,1)} async-done(((bf16[128,896]{1,0:T(8,128)(2,1)}), bf16[4096,896]{1,0:T(8,128)(2,1)}) %all-gather.9.cloned.1.call-update) | async-done | bytes 7340048 | tf_op jit(solution)/shard_map/all_gather | solution.py:26
  325.4 0.0 copy-done.1
  325.4 14.9 %fusion.6 = f32[384,4096]{1,0:T(8,128)} fusion(bf16[896,4096]{1,0:T(8,128)(2,1)} %all-gather.11.cloned.1.call-done, bf16[384,4096]{1,0:T(8,128)(2,1)S(1)} %copy-done.1, bf16[4096,896]{1,0:T(8,128)(2,1)} %all-gather.9.cloned.1.call-done, f32[384,896]{1,0:T(8,128)} %fusion.22), kind=kOutput, calls=%fused_computation.11 | convolution fusion | flops 5639208960 | bytes 25493504 | tf_op jit(solution)/shard_map/dot_general | solution.py:34
  340.2 0.0 copy-start.7
  340.2 0.0 copy-start.6
  340.2 0.0 copy-start.2
  340.2 0.0 copy-start.5
  340.3 0.0 reduce-scatter.2.cloned.1.call-update
  340.3 0.6 copy-done.7
  340.9 0.2 convert_reduce_fusion
  341.1 0.1 iota_compare_fusion.1
  341.2 0.1 fusion.15
  341.3 0.7 copy.22
  342.0 5.1 all-to-all-start.1
  347.1 0.0 copy-done.6
  347.1 0.1 convert_divide_fusion
  347.2 7.5 %all-to-all-done.1 = s32[32,1,2]{2,1,0:T(1,128)S(1)} async-done(((s32[32,1,2]{2,1,0:T(1,128)}), s32[32,1,2]{2,1,0:T(1,128)S(1)}, u32[]{:S(2)}, u32[]{:S(2)}) %all-to-all-start.1) | async-done | bytes 288 | tf_op jit(solution)/shard_map/all_to_all | solution.py:59
  354.8 0.1 copy.23
  354.8 0.1 copy.26
  354.9 0.1 reshape.125
  355.0 138.2 %reduce-scatter.2.cloned.1.call-done = f32[384,512]{1,0:T(8,128)} async-done(((f32[384,4096]{1,0:T(8,128)}), f32[384,512]{1,0:T(8,128)}) %reduce-scatter.2.cloned.1.call-update) | async-done | bytes 786448 | tf_op jit(solution)/shard_map/reduce_scatter | solution.py:39
  493.2 0.0 copy-done.2
  493.2 1.3 fusion.3
  494.6 0.1 fusion.10
  494.7 22.0 %psum.7 = f32[24]{0:T(128)S(1)} all-reduce(f32[24]{0:T(128)S(1)} %fusion.10), channel_id=1, replica_groups=mesh['list'=32,'tensor'=8] {'tensor'}, use_global_device_ids=true, to_apply=%region_3.4 | all-reduce | flops 24 | bytes 192 | tf_op jit(solution)/shard_map/psum | solution.py:42
  516.7 0.0 copy-done.5
  516.7 0.1 fusion.11
  516.8 0.0 copy-start.3
  516.8 0.4 fusion.8
  517.2 0.7 copy.21
  517.9 8.2 %all-to-all-start = ((f32[32,2,512]{2,1,0:T(2,128)}), f32[32,2,512]{2,1,0:T(2,128)S(1)}, u32[]{:S(2)}, u32[]{:S(2)}) async-start(f32[32,2,512]{2,1,0:T(2,128)} %copy.21), calls=%async_computation.1 | async-start | bytes 262144 | tf_op jit(solution)/shard_map/all_to_all | solution.py:58
  526.2 3.4 gather_fusion
  529.7 0.1 copy.24
  529.8 5.1 all-to-all-done
  534.8 0.1 convert_subtract_fusion
  535.0 12.1 %all_to_all.25 = f32[32,2,512]{2,1,0:T(2,128)S(1)} all-to-all(f32[32,2,512]{2,1,0:T(2,128)S(1)} %convert_subtract_fusion), channel_id=1, replica_groups=mesh['list'=32,'tensor'=8] {'list'}, dimensions={0} | all-to-all | bytes 262144 | tf_op jit(solution)/shard_map/all_to_all | solution.py:61
  547.1 0.9 convolution_bitcast_fusion
  548.1 0.0 copy-done.3
  (9 shorter events, 0.1 us)
Async XLA Ops:
  7.2 102.6 %copy-start.4 = (f32[4096]{0:T(1024)S(1)}, f32[4096]{0:T(1024)}, u32[]{:S(2)}) copy-start(f32[4096]{0:T(1024)} %param.12) | copy-start | bytes 49156
  7.2 99.8 %all-gather.5.cloned.1.call-start = ((), (), s32[]{:S(2)}) async-start(), calls=%async_computation.4 | async-start | bytes 3538944 | tf_op jit(solution)/shard_map/all_gather | solution.py:13
  7.9 165.1 %all-gather.7.cloned.1.call-start = ((), (), s32[]{:S(2)}) async-start(), calls=%async_computation.5 | async-start | bytes 7569408 | tf_op jit(solution)/shard_map/all_gather | solution.py:21
  8.7 247.8 %all-gather.11.cloned.1.call-start = ((), (), s32[]{:S(2)}) async-start(), calls=%async_computation.7 | async-start | bytes 7569408 | tf_op jit(solution)/shard_map/all_gather | solution.py:36
  9.4 316.0 %all-gather.9.cloned.1.call-start = ((), (), s32[]{:S(2)}) async-start(), calls=%async_computation.6 | async-start | bytes 7569408 | tf_op jit(solution)/shard_map/all_gather | solution.py:26
  10.0 483.3 %reduce-scatter.2.cloned.1.call-start = ((), (), s32[]{:S(2)}) async-start(), calls=%async_computation.8 | async-start | bytes 7077888 | tf_op jit(solution)/shard_map/reduce_scatter | solution.py:39
  106.9 2.8 copy-start
  112.5 212.9 %copy-start.1 = (bf16[384,4096]{1,0:T(8,128)(2,1)S(1)}, bf16[384,4096]{1,0:T(8,128)(2,1)}, u32[]{:S(2)}) copy-start(bf16[384,4096]{1,0:T(8,128)(2,1)} %fusion.1) | copy-start | bytes 9437188
  340.2 0.7 copy-start.7
  340.2 6.9 %copy-start.6 = (s32[24]{0:T(128)S(1)}, s32[24]{0:T(128)}, u32[]{:S(2)}) copy-start(s32[24]{0:T(128)} %param.10) | copy-start | bytes 292
  340.2 153.0 %copy-start.2 = (bf16[24,16,512]{2,1,0:T(8,128)(2,1)S(1)}, bf16[24,16,512]{2,1,0:T(8,128)(2,1)}, u32[]{:S(2)}) copy-start(bf16[24,16,512]{2,1,0:T(8,128)(2,1)} %param.9) | copy-start | bytes 1179652
  340.2 176.5 %copy-start.5 = (f32[512]{0:T(512)S(1)}, f32[512]{0:T(512)}, u32[]{:S(2)}) copy-start(f32[512]{0:T(512)} %param.16) | copy-start | bytes 6148
  342.0 12.8 %all-to-all-start.1 = ((s32[32,1,2]{2,1,0:T(1,128)}), s32[32,1,2]{2,1,0:T(1,128)S(1)}, u32[]{:S(2)}, u32[]{:S(2)}) async-start(s32[32,1,2]{2,1,0:T(1,128)} %copy.22), calls=%async_computation.2 | async-start | bytes 32768 | tf_op jit(solution)/shard_map/all_to_all | solution.py:59
  516.8 31.3 %copy-start.3 = (f32[24,512]{1,0:T(8,128)}, f32[24,512]{1,0:T(8,128)S(1)}, u32[]{:S(2)}) copy-start(f32[24,512]{1,0:T(8,128)S(1)} %fusion.11) | copy-start | bytes 147460
  517.9 16.9 %all-to-all-start = ((f32[32,2,512]{2,1,0:T(2,128)}), f32[32,2,512]{2,1,0:T(2,128)S(1)}, u32[]{:S(2)}, u32[]{:S(2)}) async-start(f32[32,2,512]{2,1,0:T(2,128)} %copy.21), calls=%async_computation.1 | async-start | bytes 262144 | tf_op jit(solution)/shard_map/all_to_all | solution.py:58
Sparse Core Ops, SparseCore 0:
  10.5 96.4 all-gather.4
  108.8 64.2 all-gather.6
  174.8 81.5 all-gather.10
  258.2 67.1 all-gather.8
  340.4 152.7 reduce-scatter.1
where the time goes:
time: 559 us; the launch traced here: 555 us
  waiting for transfers between devices  455 us (81%)
  blocking collectives  34.1 us (6%)
  matrix products  26.1 us (5%)
  between operations  13.9 us (2%)
  starting transfers between devices  13.5 us (2%)
  other arithmetic  6.25 us (1%)
  local copies, waits for them, and re-layouts  6.05 us (1%)
    reduce_scatter x1, waiting for transfers between devices, per_device(): mixed = lax.psum_scatter(terms, 'tensor', scatter_dimension=1, tiled=True)  138 us
    all_gather x1, waiting for transfers between devices, per_device(): whole = lax.all_gather(states, 'tensor', axis=2, tiled=True)  96.9 us
    all_gather x1, waiting for transfers between devices, per_device(): lax.all_gather(down_weight, 'list', axis=1, tiled=True)  74.8 us
    all_gather x1, waiting for transfers between devices, per_device(): lax.all_gather(up_weight, 'list', axis=0, tiled=True)  68.9 us
    all_gather x1, waiting for transfers between devices, per_device(): lax.all_gather(gate_weight, 'list', axis=0, tiled=True)  60.5 us
    psum x1, blocking collectives, per_device(): total = lax.psum(jnp.sum(pooled * pooled, axis=1), 'tensor')  22 us
    dot_general x1, matrix products, per_device(): jnp.dot(hidden, lax.all_gather(down_weight, 'list', axis=1, tiled=True),...  14.9 us
    all_to_all x1, blocking collectives, per_device(): lax.all_to_all(differences, 'list', split_axis=0, concat_axis=0, tiled=True)  12.1 us
  transfers between devices with their start and end apart: 7, of which 7 were waited for; matrix products, arithmetic and copies ran while one was open for 3% of the time, Pallas kernels for 0%

commit v1 on v0

v1 whole, which is shorter than its diff:
```python
import jax
import jax.numpy as jnp
from jax import lax
from jax.sharding import PartitionSpec as P

CAP = 2


def per_device(
    states, lengths, assign, norm_gain, gate_weight, up_weight, down_weight, out_gain, centroids
):
    passes, seq, width_part = states.shape
    n_list = lax.axis_size("list")
    n_tensor = lax.axis_size("tensor")
    per_owner = centroids.shape[0]
    down_part = down_weight.shape[1]
    me = lax.axis_index("list")
    everyone = lax.all_gather(assign, "list", axis=0)
    mine = everyone // per_owner == me
    rank = jnp.cumsum(mine.astype(jnp.int32), axis=1) - 1
    slot_hit = mine[:, None, :] & (rank[:, None, :] == jnp.arange(CAP, dtype=jnp.int32)[None, :, None])
    local = jnp.sum(jnp.where(slot_hit, (everyone - me * per_owner)[:, None, :], 0), axis=2)
    rows = jnp.take(centroids, local, axis=0)
    back = lax.all_to_all(rows, "list", split_axis=0, concat_axis=0, tiled=True)
    owner = assign // per_owner
    places = jnp.arange(passes, dtype=jnp.int32)
    same_owner = owner[:, None] == owner[None, :]
    earlier = places[:, None] > places[None, :]
    my_rank = jnp.sum((same_owner & earlier).astype(jnp.int32), axis=1)
    pick = (owner * CAP + my_rank)[:, None] == jnp.arange(n_list * CAP, dtype=jnp.int32)[None, :]
    chosen = jnp.dot(
        pick.astype(jnp.bfloat16),
        back.reshape(n_list * CAP, width_part),
        preferred_element_type=jnp.float32,
    )

    whole = lax.all_gather(states, "tensor", axis=2, tiled=True)
    width = whole.shape[2]
    rows_n = passes * seq
    flat = whole.reshape(rows_n, width).astype(jnp.float32)
    scale = lax.rsqrt(jnp.mean(flat * flat, axis=1, keepdims=True) + 1e-05)
    normed = (flat * scale * norm_gain[None, :]).astype(jnp.bfloat16)
    gate = jnp.dot(
        normed,
        lax.all_gather(gate_weight, "list", axis=0, tiled=True),
        preferred_element_type=jnp.float32,
    )
    up = jnp.dot(
        normed,
        lax.all_gather(up_weight, "list", axis=0, tiled=True),
        preferred_element_type=jnp.float32,
    )
    hidden = jax.nn.silu(gate) * up
    slots = jnp.arange(seq, dtype=jnp.int32)
    valid = (slots[None, :] < lengths[:, None]).astype(jnp.float32)
    pool_w = valid / lengths[:, None].astype(jnp.float32)
    pool_hidden = jnp.sum(hidden.reshape(passes, seq, -1) * pool_w[:, :, None], axis=1)
    pool_states = jnp.sum(states.astype(jnp.float32) * pool_w[:, :, None], axis=1)
    all_hidden = lax.all_gather(pool_hidden.astype(jnp.bfloat16), "list", axis=0, tiled=True)
    terms = jnp.dot(all_hidden, down_weight, preferred_element_type=jnp.float32)
    terms = terms.reshape(n_list, passes, down_part)
    part = lax.psum_scatter(terms, "tensor", scatter_dimension=0, tiled=True)
    per = n_list // n_tensor
    t = lax.axis_index("tensor")
    gathered = lax.all_gather(part, "list", axis=0)
    full = gathered.transpose(1, 2, 0, 3).reshape(per, passes, n_tensor, width_part)
    mine_out = lax.all_to_all(full, "tensor", split_axis=2, concat_axis=0, tiled=True)
    mixed = mine_out.reshape(n_list, passes, width_part)
    mixed = lax.dynamic_index_in_dim(mixed, me, axis=0, keepdims=False)
    pooled = pool_states + mixed
    total = lax.psum(jnp.sum(pooled * pooled, axis=1), "tensor")
    embedding = pooled * lax.rsqrt(total[:, None] / width + 1e-05) * out_gain[None, :]
    residual = embedding - chosen
    return (embedding, residual)


def solution(mesh):
    return jax.shard_map(
        per_device,
        mesh=mesh,
        in_specs=(
            P("list", None, "tensor"),
            P("list"),
            P("list"),
            P(),
            P("list", "tensor"),
            P("list", "tensor"),
            P("tensor", "list"),
            P("tensor"),
            P("list", "tensor"),
        ),
        out_specs=(P("list", "tensor"), P("list", "tensor")),
        check_vma=False,
    )
```

time: 559 us -> 540 us (0.966)
  waiting for transfers between devices: 455 us -> 422 us
  blocking collectives: 34.1 us -> 42.3 us
  matrix products: 26.1 us -> 18.9 us
    reduce_scatter x1, waiting for transfers between devices: 138 us -> 83.8 us  [per_device(): part = lax.psum_scatter(terms, 'tensor', scatter_dimension=0, tiled=True)]
    all_gather x1 -> x2, waiting for transfers between devices: 74.8 us -> 91.4 us  [the longest x1 58.4 us: per_device(): lax.all_gather(pool_hidden.astype(jnp.bfloat16), 'list', axis=0, tiled=True)]
    all_to_all x2, waiting for transfers between devices: 12.6 us -> 27.7 us  [the longest x1 27.7 us: per_device(): lax.all_to_all(full, 'tensor', split_axis=2, concat_axis=0, tiled=True)]
    unnamed x0 -> x1, blocking collectives: none -> 13.7 us
    all_to_all x1 -> x0, blocking collectives: 12.1 us -> none  [per_device(): lax.all_to_all(differences, 'list', split_axis=0, concat_axis=0, tiled=True)]
    all_gather x1, waiting for transfers between devices: 68.9 us -> 60.3 us  [per_device(): lax.all_gather(up_weight, 'list', axis=0, tiled=True)]
    dot_general x4 -> x3, matrix products: 17.5 us -> 10.3 us  [the longest x1 6.88 us: per_device(): jnp.dot(normed, lax.all_gather(up_weight, 'list', axis=0, tiled=True), pr...]
    psum x1, blocking collectives: 22 us -> 28.6 us  [per_device(): total = lax.psum(jnp.sum(pooled * pooled, axis=1), 'tensor')]
  transfers between devices with their start and end apart: 7 -> 8, of which waited for: 7 -> 7; matrix products, arithmetic and copies ran while one was open for 3% -> 5% of each run, Pallas kernels for 0% -> 0%
where the time goes in v1:
time: 540 us; the launch traced here: 531 us
  waiting for transfers between devices  422 us (78%)
  blocking collectives  42.3 us (8%)
  matrix products  18.9 us (3%)
  between operations  15 us (3%)
  starting transfers between devices  13.4 us (2%)
  local copies, waits for them, and re-layouts  9.79 us (2%)
  other arithmetic  9.4 us (2%)
    all_gather x1, waiting for transfers between devices, per_device(): whole = lax.all_gather(states, 'tensor', axis=2, tiled=True)  96.1 us
    reduce_scatter x1, waiting for transfers between devices, per_device(): part = lax.psum_scatter(terms, 'tensor', scatter_dimension=0, tiled=True)  83.8 us
    all_gather x1, waiting for transfers between devices, per_device(): lax.all_gather(gate_weight, 'list', axis=0, tiled=True)  60.6 us
    all_gather x1, waiting for transfers between devices, per_device(): lax.all_gather(up_weight, 'list', axis=0, tiled=True)  60.3 us
    all_gather x1, waiting for transfers between devices, per_device(): lax.all_gather(pool_hidden.astype(jnp.bfloat16), 'list', axis=0, tiled=True)  58.4 us
    all_gather x1, waiting for transfers between devices, per_device(): gathered = lax.all_gather(part, 'list', axis=0)  33 us
    psum x1, blocking collectives, per_device(): total = lax.psum(jnp.sum(pooled * pooled, axis=1), 'tensor')  28.6 us
    all_to_all x1, waiting for transfers between devices, per_device(): lax.all_to_all(full, 'tensor', split_axis=2, concat_axis=0, tiled=True)  27.7 us
  transfers between devices with their start and end apart: 8, of which 7 were waited for; matrix products, arithmetic and copies ran while one was open for 5% of the time, Pallas kernels for 0%

profile of v1, /device:TPU:6, one launch (start us, length us, event | category | flops | bytes accessed | tf_op | source)
XLA Modules:
  0.0 530.8 jit_solution(11270242722091826068)
XLA Ops:
  7.2 0.0 copy-start
  7.2 0.0 copy-start.5
  7.2 0.0 all-gather.8.cloned.1.call-start
  7.2 0.7 all-gather.8.cloned.1.call-update
  7.9 0.0 all-gather.10.cloned.1.call-start
  8.0 0.7 all-gather.10.cloned.1.call-update
  8.7 0.0 all-gather.12.cloned.1.call-start
  8.7 0.7 all-gather.12.cloned.1.call-update
  9.4 0.0 all-gather.14.cloned.1.call-start
  9.5 0.7 convert_element_type.38
  10.1 0.7 convert_divide_fusion
  10.8 96.1 %all-gather.8.cloned.1.call-done = bf16[24,16,4096]{2,1,0:T(8,128)(2,1)} async-done(((bf16[24,16,512]{2,1,0:T(8,128)(2,1)}), bf16[24,16,4096]{2,1,0:T(8,128)(2,1)}) %all-gather.8.cloned.1.call-update) | async-done | bytes 3145744 | tf_op jit(solution)/shard_map/all_gather | solution.py:37
  107.0 2.7 multiply_reduce_fusion
  109.7 0.1 rsqrt.16
  109.8 0.0 copy-done.5
  109.8 0.0 copy-done.1
  109.8 2.7 fusion.1
  112.5 60.6 %all-gather.10.cloned.1.call-done = bf16[4096,896]{1,0:T(8,128)(2,1)} async-done(((bf16[128,896]{1,0:T(8,128)(2,1)}), bf16[4096,896]{1,0:T(8,128)(2,1)}) %all-gather.10.cloned.1.call-update) | async-done | bytes 7340048 | tf_op jit(solution)/shard_map/all_gather | solution.py:45
  173.1 8.5 %fusion.10 = f32[384,896]{1,0:T(8,128)} fusion(bf16[384,4096]{1,0:T(8,128)(2,1)} %fusion.1, bf16[4096,896]{1,0:T(8,128)(2,1)} %all-gather.10.cloned.1.call-done), kind=kOutput, calls=%fused_computation.45 | convolution fusion | flops 2818572288 | bytes 11862016 | tf_op jit(solution)/shard_map/dot_general | solution.py:43
  181.6 60.3 %all-gather.12.cloned.1.call-done = bf16[4096,896]{1,0:T(8,128)(2,1)} async-done(((bf16[128,896]{1,0:T(8,128)(2,1)}), bf16[4096,896]{1,0:T(8,128)(2,1)}) %all-gather.12.cloned.1.call-update) | async-done | bytes 7340048 | tf_op jit(solution)/shard_map/all_gather | solution.py:50
  241.9 0.0 copy-done.2
  241.9 6.9 %convolution_multiply_fusion = f32[384,896]{1,0:T(8,128)S(1)} fusion(bf16[384,4096]{1,0:T(8,128)(2,1)S(1)} %copy-done.2, bf16[4096,896]{1,0:T(8,128)(2,1)} %all-gather.12.cloned.1.call-done, f32[384,896]{1,0:T(8,128)} %fusion.10), kind=kOutput, calls=%fused_computation.5 | convolution fusion | flops 2820292608 | bytes 13238272 | tf_op jit(solution)/shard_map/dot_general | solution.py:48
  248.8 0.0 copy-start.8
  248.8 0.0 copy-start.7
  248.8 0.9 multiply_reduce_fusion.1
  249.7 0.0 all-gather.14.cloned.1.call-update
  249.8 0.0 reduce-scatter.2.cloned.1.call-start
  249.8 58.4 %all-gather.14.cloned.1.call-done = bf16[768,896]{1,0:T(8,128)(2,1)} async-done(((bf16[24,896]{1,0:T(8,128)(2,1)}), bf16[768,896]{1,0:T(8,128)(2,1)}) %all-gather.14.cloned.1.call-update) | async-done | bytes 1376272 | tf_op jit(solution)/shard_map/all_gather | solution.py:59
  308.2 0.0 copy-done
  308.2 2.6 fusion.11
  310.8 0.0 reduce-scatter.2.cloned.1.call-update
  310.9 0.0 all-gather.16.cloned.1.call-start
  310.9 83.8 %reduce-scatter.2.cloned.1.call-done = f32[4,24,128]{2,1,0:T(8,128)} async-done(((f32[32,24,128]{2,1,0:T(8,128)}), f32[4,24,128]{2,1,0:T(8,128)}) %reduce-scatter.2.cloned.1.call-update) | async-done | bytes 49168 | tf_op jit(solution)/shard_map/reduce_scatter | solution.py:62
  394.7 0.0 all-gather.16.cloned.1.call-update
  394.8 0.6 dynamic-slice
  396.0 0.0 copy-done.7
  396.0 0.2 dynamic-update-slice
  396.3 13.7 %all-reduce = s32[768]{0:T(1024)S(1)} all-reduce(s32[768]{0:T(1024)S(1)} %dynamic-update-slice), channel_id=3, replica_groups=mesh['list'=32,'tensor'=8] {'list'}, use_global_device_ids=true, to_apply=%add | all-reduce | flops 768 | bytes 6144
  410.0 0.1 reshape.130
  410.1 0.2 reduce_window_sum.11
  410.3 0.1 copy.26
  410.4 0.1 copy.25
  410.5 0.1 copy.27
  410.6 0.1 copy.29
  410.7 0.1 reshape.123
  410.8 3.5 gather_fusion
  414.3 0.1 copy.28
  414.4 0.8 broadcast_select_fusion
  415.2 5.0 all-to-all-start.1
  420.2 33.0 %all-gather.16.cloned.1.call-done = f32[128,24,128]{2,1,0:T(8,128)} async-done(((f32[4,24,128]{2,1,0:T(8,128)}), f32[128,24,128]{2,1,0:T(8,128)}) %all-gather.16.cloned.1.call-update) | async-done | bytes 1572880 | tf_op jit(solution)/shard_map/all_gather | solution.py:65
  453.2 2.3 copy.23
  455.5 0.2 reshape.117
  455.8 0.0 copy-start.6
  455.8 2.1 copy.24
  457.9 0.0 all-to-all-done.1
  457.9 8.2 %all-to-all-start = ((f32[4,24,8,512]{3,1,0,2:T(8,128)}), f32[4,24,8,512]{3,1,0,2:T(8,128)S(1)}, u32[]{:S(2)}, u32[]{:S(2)}) async-start(f32[4,24,8,512]{3,1,0,2:T(8,128)} %copy.24), calls=%async_computation.1 | async-start | bytes 3145728 | tf_op jit(solution)/shard_map/all_to_all | solution.py:67
  466.1 0.2 convert_reduce_fusion
  466.3 0.3 multiply_reduce_fusion.2
  466.6 27.7 %all-to-all-done = f32[4,24,8,512]{3,1,0,2:T(8,128)S(1)} async-done(((f32[4,24,8,512]{3,1,0,2:T(8,128)}), f32[4,24,8,512]{3,1,0,2:T(8,128)S(1)}, u32[]{:S(2)}, u32[]{:S(2)}) %all-to-all-start) | async-done | bytes 1572896 | tf_op jit(solution)/shard_map/all_to_all | solution.py:67
  494.3 0.1 multiply_reduce_fusion.3
  494.4 28.6 %psum.7 = f32[24]{0:T(128)S(1)} all-reduce(f32[24]{0:T(128)S(1)} %multiply_reduce_fusion.3), channel_id=1, replica_groups=mesh['list'=32,'tensor'=8] {'tensor'}, use_global_device_ids=true, to_apply=%region_5.6 | all-reduce | flops 24 | bytes 192 | tf_op jit(solution)/shard_map/psum | solution.py:71
  523.1 0.1 multiply_multiply_fusion
  523.2 0.8 convolution_subtract_fusion
  524.0 0.0 copy-done.4
  (21 shorter events, 0.2 us)
Async XLA Ops:
  7.2 301.0 %copy-start = (bf16[896,128]{1,0:T(8,128)(2,1)S(1)}, bf16[896,128]{1,0:T(8,128)(2,1)}, u32[]{:S(2)}) copy-start(bf16[896,128]{1,0:T(8,128)(2,1)} %param.15) | copy-start | bytes 688132
  7.2 102.6 %copy-start.5 = (f32[4096]{0:T(1024)S(1)}, f32[4096]{0:T(1024)}, u32[]{:S(2)}) copy-start(f32[4096]{0:T(1024)} %param.12) | copy-start | bytes 49156
  7.2 99.8 %all-gather.8.cloned.1.call-start = ((), (), s32[]{:S(2)}) async-start(), calls=%async_computation.3 | async-start | bytes 3538944 | tf_op jit(solution)/shard_map/all_gather | solution.py:37
  7.9 165.1 %all-gather.10.cloned.1.call-start = ((), (), s32[]{:S(2)}) async-start(), calls=%async_computation.4 | async-start | bytes 7569408 | tf_op jit(solution)/shard_map/all_gather | solution.py:45
  8.7 233.2 %all-gather.12.cloned.1.call-start = ((), (), s32[]{:S(2)}) async-start(), calls=%async_computation.5 | async-start | bytes 7569408 | tf_op jit(solution)/shard_map/all_gather | solution.py:50
  9.4 298.8 %all-gather.14.cloned.1.call-start = ((), (), s32[]{:S(2)}) async-start(), calls=%async_computation.6 | async-start | bytes 1419264 | tf_op jit(solution)/shard_map/all_gather | solution.py:59
  106.9 2.8 copy-start.1
  112.5 129.4 %copy-start.2 = (bf16[384,4096]{1,0:T(8,128)(2,1)S(1)}, bf16[384,4096]{1,0:T(8,128)(2,1)}, u32[]{:S(2)}) copy-start(bf16[384,4096]{1,0:T(8,128)(2,1)} %fusion.1) | copy-start | bytes 9437188
  248.8 146.0 %copy-start.8 = (u32[256]{0:T(256)S(1)}, u32[256]{0:T(256)}, u32[]{:S(2)}) copy-start(u32[256]{0:T(256)} %constant.76) | copy-start | bytes 3076
  248.8 147.2 %copy-start.7 = (s32[24]{0:T(128)S(1)}, s32[24]{0:T(128)}, u32[]{:S(2)}) copy-start(s32[24]{0:T(128)} %param.11) | copy-start | bytes 292
  249.8 145.0 %reduce-scatter.2.cloned.1.call-start = ((), (), s32[]{:S(2)}) async-start(), calls=%async_computation.7 | async-start | bytes 442368 | tf_op jit(solution)/shard_map/reduce_scatter | solution.py:62
  310.9 142.3 %all-gather.16.cloned.1.call-start = ((), (), s32[]{:S(2)}) async-start(), calls=%async_computation.8 | async-start | bytes 1622016 | tf_op jit(solution)/shard_map/all_gather | solution.py:65
  415.2 42.7 %all-to-all-start.1 = ((bf16[32,2,512]{2,1,0:T(2,128)(2,1)}), bf16[32,2,512]{2,1,0:T(2,128)(2,1)S(1)}, u32[]{:S(2)}, u32[]{:S(2)}) async-start(bf16[32,2,512]{2,1,0:T(2,128)(2,1)} %broadcast_select_fusion), calls=%async_computation.2 | async-start | bytes 131072 | tf_op jit(solution)/shard_map/all_to_all | solution.py:24
  455.8 67.3 %copy-start.6 = (f32[512]{0:T(512)S(1)}, f32[512]{0:T(512)}, u32[]{:S(2)}) copy-start(f32[512]{0:T(512)} %param.16) | copy-start | bytes 6148
  457.9 8.4 %copy-start.3 = (bf16[24,16,512]{2,1,0:T(8,128)(2,1)S(1)}, bf16[24,16,512]{2,1,0:T(8,128)(2,1)}, u32[]{:S(2)}) copy-start(bf16[24,16,512]{2,1,0:T(8,128)(2,1)} %param.9) | copy-start | bytes 1179652
  457.9 36.5 %all-to-all-start = ((f32[4,24,8,512]{3,1,0,2:T(8,128)}), f32[4,24,8,512]{3,1,0,2:T(8,128)S(1)}, u32[]{:S(2)}, u32[]{:S(2)}) async-start(f32[4,24,8,512]{3,1,0,2:T(8,128)} %copy.24), calls=%async_computation.1 | async-start | bytes 3145728 | tf_op jit(solution)/shard_map/all_to_all | solution.py:67
  523.2 0.8 copy-start.4
Sparse Core Ops, SparseCore 0:
  10.5 96.4 all-gather.7
  108.8 64.2 all-gather.9
  174.9 66.9 all-gather.11
  249.9 58.2 all-gather.13
  311.9 82.7 reduce-scatter.1
  396.5 56.6 all-gather.15

commit v2 on v0

v2 whole, which is shorter than its diff:
```python
import functools

import jax
import jax.numpy as jnp
from jax import lax
from jax.experimental import pallas as pl
from jax.experimental.pallas import tpu as pltpu
from jax.sharding import PartitionSpec as P

MESH = pl.DeviceIdType.MESH
BF = jnp.bfloat16
F32 = jnp.float32

PASSES, SEQ, PART, WIDTH = 24, 16, 512, 4096
ROWS = PASSES * SEQ
HID = 896
TILES = HID // 128
PAD = 32
OWN_ROWS = 4096

R_Z = 0
R_Y = 4
R_H = 12
R_SC = 20
R_SY = 24
R_SH = 32
R_DN = 40
R_CR = 44
R_X = 46
R_G = 62
R_1 = 70
R_2 = 74
R_3 = 82
R_END = 90
N_SEND = 96


def kernel(
    lengths, assign, states, gain, gate, up, down, out_gain, centroids,
    emb_out, res_out,
    wbuf, xbuf, acc, cbuf, dbuf, sbuf, g_in, u_in, gain_in, og_in,
    scale_s, mask_s, inv_s, hb, tf, tb, r1b, qs, rb, sb, abuf, pick, cacc, resp, gotc, chosen_s, smean,
    ss, rs, ls, req_s, req_r, rsp_s, rsp_r,
):
    lst = lax.axis_index("list")
    ten = lax.axis_index("tensor")
    core = lax.rem(lst, 2)
    y = lax.rem(lst // 2, 4)
    zl = lst // 8
    x = ten // 2
    zh = lax.rem(ten, 2)
    me_g = lax.rem(lst, 8)

    def dev(list_=None, tensor=None):
        return {"list": lst if list_ is None else list_, "tensor": ten if tensor is None else tensor}

    def at_z(z):
        return dev(list_=z * 8 + me_g)

    def at_y(step):
        return dev(list_=zl * 8 + lax.rem(y + step + 4, 4) * 2 + core)

    def at_x(step):
        return dev(tensor=lax.rem(x + step + 4, 4) * 2 + zh)

    sibling = dev(list_=lst + 1 - 2 * core)
    partner = dev(tensor=x * 2 + 1 - zh)

    sends = []

    def send(src, dst, recv, device, cond=None):
        n = len(sends)
        cp = pltpu.make_async_remote_copy(
            src_ref=src, dst_ref=dst, send_sem=ss.at[n], recv_sem=rs.at[recv],
            device_id=device, device_id_type=MESH,
        )
        sends.append((cp, cond))
        if cond is None:
            cp.start()
        else:
            pl.when(cond)(cp.start)

    def arrived(dst, recv):
        pltpu.make_async_remote_copy(
            src_ref=dst, dst_ref=dst, send_sem=ss.at[0], recv_sem=rs.at[recv],
            device_id=sibling, device_id_type=MESH,
        ).wait_recv()

    locals_ = []

    def local(src, dst):
        cp = pltpu.make_async_copy(src, dst, ls.at[len(locals_)])
        locals_.append(cp)
        cp.start()
        return cp

    def xslot(z_hi, half, x_):
        return xbuf.at[z_hi * 2 + half, :, pl.ds(pl.multiple_of(x_ * 256, 256), 256)]

    cps_w = [local(gate, g_in), local(up, u_in), local(gain, gain_in)]
    for half in range(2):
        send(states.at[:, pl.ds(half * 256, 256)], xslot(zh, half, x), R_CR + half, partner)
    for step in (1, -1, 2):
        for half in range(2):
            send(states.at[:, pl.ds(half * 256, 256)], xslot(zh, half, x), R_X + x * 2 + half, at_x(step))
    cps_x = [local(states.at[:, pl.ds(half * 256, 256)], xslot(zh, half, x)) for half in range(2)]

    for cp in cps_w:
        cp.wait()
    eye = lax.broadcasted_iota(jnp.int32, (128, 128), 0) == lax.broadcasted_iota(jnp.int32, (128, 128), 1)
    gcol = jnp.sum(jnp.where(eye, gain_in[pl.ds(lst, 1), :], 0.0), axis=1, keepdims=True)
    own_rows = pl.ds(pl.multiple_of(zl * 256 + core * 128, 128), 128)
    for j in range(TILES):
        wbuf[y, own_rows, j * 256 : j * 256 + 128] = (g_in[:, j * 128 : j * 128 + 128].astype(F32) * gcol).astype(BF)
        wbuf[y, own_rows, j * 256 + 128 : j * 256 + 256] = (u_in[:, j * 128 : j * 128 + 128].astype(F32) * gcol).astype(BF)

    def wblock(y_, z_, c_, start=0, rows=128):
        return wbuf.at[y_, pl.ds(pl.multiple_of(z_ * 256 + c_ * 128 + start, 64), rows)]

    def place(k):
        inner = (zl == 1) | (zl == 2)
        o = jnp.where(inner, 1 - k, k) if k < 2 else k
        return jnp.where(zl < 2, o, 3 - o)

    def y_of(step):
        return lax.rem(y + step + 4, 4)

    def column(k):
        z_ = place(k)
        block = wblock(y, z_, core)
        if k == 0:
            send(block, block, R_Z + z_, at_z(lax.rem(zl + 1, 4)), zl < 3)
            send(block, block, R_Z + z_, at_z(lax.rem(zl + 3, 4)), zl > 0)
        else:
            arrived(block, R_Z + z_)
            onward = jnp.where(z_ < zl, zl + 1, zl - 1)
            there = (onward >= 0) & (onward < 4)
            send(block, block, R_Z + z_, at_z(lax.rem(onward + 4, 4)), there)
        send(block, block, R_Y + k, at_y(1))
        send(block, block, R_Y + 4 + k, at_y(-1))
        send(block, block, R_SC + k, sibling)

    def neighbour(k):
        z_ = place(k)
        for d, step in ((0, -1), (1, 1)):
            block = wblock(y_of(step), z_, core)
            arrived(block, R_Y + d * 4 + k)
            part = wblock(y_of(step), z_, core, d * 64, 64)
            send(part, part, R_H + d * 4 + k, at_y(-step))
            send(block, block, R_SY + d * 4 + k, sibling)

    def halves(k):
        z_ = place(k)
        for d in range(2):
            part = wblock(y_of(2), z_, core, d * 64, 64)
            arrived(part, R_H + d * 4 + k)
            send(part, part, R_SH + d * 4 + k, sibling)

    def dslot(z_):
        return dbuf.at[:, pl.ds(pl.multiple_of(z_ * 128, 128), 128)]

    def down_column(k):
        z_ = place(k)
        if k == 0:
            send(down, dslot(z_), R_DN + z_, at_z(lax.rem(zl + 1, 4)), zl < 3)
            send(down, dslot(z_), R_DN + z_, at_z(lax.rem(zl + 3, 4)), zl > 0)
        else:
            arrived(dslot(z_), R_DN + z_)
            onward = jnp.where(z_ < zl, zl + 1, zl - 1)
            there = (onward >= 0) & (onward < 4)
            send(dslot(z_), dslot(z_), R_DN + z_, at_z(lax.rem(onward + 4, 4)), there)

    column(0)

    cp_d = local(down, dslot(zl))
    cp_s = local(states, sbuf)
    cp_c = local(centroids, cbuf)
    cp_o = local(out_gain, og_in)
    lane = lax.broadcasted_iota(jnp.int32, (1, 128), 1)
    arow = jnp.full((1, 128), -1, jnp.int32)
    sub = lax.broadcasted_iota(jnp.int32, (PAD, 128), 0)
    acol = jnp.full((PAD, 128), -1, jnp.int32)
    lcol = jnp.ones((PAD, 128), jnp.int32)
    for p in range(PASSES):
        arow = jnp.where(lane == p, assign[p], arow)
        acol = jnp.where(sub == p, assign[p], acol)
        lcol = jnp.where(sub == p, lengths[p], lcol)
    abuf[lst] = arow

    def req_copy(i):
        peer = lax.rem(lst + i, 32)
        return pltpu.make_async_remote_copy(
            src_ref=abuf.at[lst], dst_ref=abuf.at[lst], send_sem=req_s.at[peer], recv_sem=req_r.at[lst],
            device_id=dev(list_=peer), device_id_type=MESH,
        )

    pl.loop(1, 32)(lambda i: req_copy(i).start())

    slot_row = lax.broadcasted_iota(jnp.int32, (PAD, ROWS), 0)
    slot_col = lax.broadcasted_iota(jnp.int32, (PAD, ROWS), 1)
    length = lcol[:, :1]
    in_pass = (slot_col >= slot_row * SEQ) & (slot_col < slot_row * SEQ + length) & (slot_row < PASSES)
    mask_s[...] = jnp.where(in_pass, 1.0, 0.0).astype(BF)
    inv_s[...] = 1.0 / lcol.astype(F32)
    cp_s.wait()
    smean[...] = jnp.dot(mask_s[...], sbuf[...], preferred_element_type=F32) * inv_s[:, :1]

    column(1)
    neighbour(0)

    def req_from(i):
        peer = lax.rem(lst + i, 32)
        pltpu.make_async_remote_copy(
            src_ref=abuf.at[peer], dst_ref=abuf.at[peer], send_sem=req_s.at[peer], recv_sem=req_r.at[peer],
            device_id=sibling, device_id_type=MESH,
        ).wait_recv()

    pl.loop(1, 32)(req_from)
    cp_c.wait()
    wanted = jnp.broadcast_to(abuf[...], (32, 8, 128))
    lanes3 = lax.broadcasted_iota(jnp.int32, (32, 8, 128), 2)
    odd3 = lax.rem(lax.broadcasted_iota(jnp.int32, (32, 8, 128), 1), 2) == 1
    mine = (wanted >= lst * OWN_ROWS) & (wanted < lst * OWN_ROWS + OWN_ROWS)
    first = jnp.min(jnp.where(mine, lanes3, 128), axis=2, keepdims=True)
    last = jnp.max(jnp.where(mine, lanes3, -1), axis=2, keepdims=True)
    chosen_lane = jnp.where(odd3, last, first)
    hit = mine & (lanes3 == chosen_lane)
    ids = jnp.sum(jnp.where(hit, wanted - lst * OWN_ROWS, 0), axis=2, keepdims=True)
    pick[...] = jnp.broadcast_to(ids, (32, 8, 128)).reshape(256, 128)
    cacc[...] = jnp.zeros_like(cacc)

    @pl.loop(0, 8)
    def _(kc):
        base = lax.broadcasted_iota(jnp.int32, (256, 512), 1) + kc * 512
        one = jnp.where(base == pick[:, :1], 1.0, 0.0).astype(BF)
        cacc[...] += jnp.dot(one, cbuf[pl.ds(pl.multiple_of(kc * 512, 512), 512), :], preferred_element_type=F32)

    quarter = lax.rem(lax.broadcasted_iota(jnp.int32, (256, 128), 0), 8) // 2
    out_rows = jnp.zeros((256, 128), F32)
    for q in range(4):
        out_rows = jnp.where(quarter == q, cacc[:, q * 128 : q * 128 + 128], out_rows)
    resp[...] = out_rows.reshape(32, 8, 128)
    gotc[lst] = resp[lst]

    def rsp_copy(i):
        peer = lax.rem(lst + i, 32)
        return pltpu.make_async_remote_copy(
            src_ref=resp.at[peer], dst_ref=gotc.at[lst], send_sem=rsp_s.at[peer], recv_sem=rsp_r.at[lst],
            device_id=dev(list_=peer), device_id_type=MESH,
        )

    pl.loop(1, 32)(lambda i: rsp_copy(i).start())

    column(2)
    neighbour(1)
    down_column(0)
    column(3)

    for half in range(2):
        arrived(xslot(1 - zh, half, x), R_CR + half)
        for step in (1, -1, 2):
            send(xslot(1 - zh, half, x), xslot(1 - zh, half, x), R_X + 8 + x * 2 + half, at_x(step))

    neighbour(2)
    down_column(1)
    neighbour(3)
    down_column(2)

    for cp in cps_x:
        cp.wait()
    for crossed, z_hi in ((0, zh), (1, 1 - zh)):
        for step in (1, -1, 2):
            x_ = lax.rem(x + step + 4, 4)
            for half in range(2):
                arrived(xslot(z_hi, half, x_), R_X + crossed * 8 + x_ * 2 + half)

    @pl.loop(0, ROWS // 32)
    def _(r):
        rows = pl.ds(pl.multiple_of(r * 32, 32), 32)
        total = jnp.zeros((32, 128), F32)
        for yy in range(4):
            for c in range(8):
                v = xbuf[yy, rows, c * 128 : c * 128 + 128].astype(F32)
                total = total + v * v
        mean = jnp.sum(total, axis=1, keepdims=True) / WIDTH
        scale_s[rows, :] = jnp.broadcast_to(lax.rsqrt(mean + 1e-05), (32, 128))

    def product(yy, start, depth, init):
        @pl.loop(0, TILES)
        def _(j):
            cols = pl.ds(pl.multiple_of(j * 256, 256), 256)
            ks = pl.ds(start, depth)
            r = jnp.dot(xbuf[yy, :, ks], wbuf[yy, ks, cols], preferred_element_type=F32)
            if init:
                acc[j] = r
            else:
                acc[j] += r

    for k in range(4):
        arrived(wblock(y, place(k), 1 - core), R_SC + k)
    product(y, 0, 1024, True)
    for d, step in ((0, -1), (1, 1)):
        for k in range(4):
            arrived(wblock(y_of(step), place(k), 1 - core), R_SY + d * 4 + k)
        product(y_of(step), 0, 1024, False)
    for k in range(4):
        halves(k)
        for d in range(2):
            arrived(wblock(y_of(2), place(k), 1 - core, d * 64, 64), R_SH + d * 4 + k)
        if k < 3:
            product(y_of(2), pl.multiple_of(place(k) * 256, 256), 256, False)
    down_column(3)
    cp_d.wait()
    cp_o.wait()

    yy = y_of(2)
    ks = pl.ds(pl.multiple_of(place(3) * 256, 256), 256)
    for j in range(TILES):
        r = acc[j] + jnp.dot(xbuf[yy, :, ks], wbuf[yy, ks, j * 256 : j * 256 + 256], preferred_element_type=F32)
        g = r[:, :128] * scale_s[...]
        u = r[:, 128:] * scale_s[...]
        h = (g / (1.0 + jnp.exp(-g)) * u).astype(BF)
        pooled_h = jnp.dot(mask_s[...], h, preferred_element_type=F32) * inv_s[...]
        hb[me_g, :, j * 128 : j * 128 + 128] = pooled_h.astype(BF)

    for i in range(1, 8):
        g_ = lax.rem(me_g + i, 8)
        send(hb.at[me_g], hb.at[me_g], R_G + me_g, dev(list_=zl * 8 + g_))

    def rsp_from(i):
        peer = lax.rem(lst + i, 32)
        pltpu.make_async_remote_copy(
            src_ref=gotc.at[peer], dst_ref=gotc.at[peer], send_sem=rsp_s.at[peer], recv_sem=rsp_r.at[peer],
            device_id=sibling, device_id_type=MESH,
        ).wait_recv()

    pl.loop(1, 32)(rsp_from)
    own_col = acol >> 12
    own_row = jnp.where(lane < PASSES, arow >> 12, -1)
    before = (own_col == own_row) & (lax.broadcasted_iota(jnp.int32, (PAD, 128), 1) < sub)
    slot = jnp.max(jnp.where(before, 1, 0), axis=1, keepdims=True)
    wide = lax.broadcasted_iota(jnp.int32, (PAD, 256), 1)
    table = gotc[...].reshape(256, 128).astype(BF)
    for q in range(4):
        one = jnp.where(wide == own_col[:, :1] * 8 + q * 2 + slot, 1.0, 0.0).astype(BF)
        chosen_s[:, q * 128 : q * 128 + 128] = jnp.dot(one, table, preferred_element_type=F32)

    for i in range(1, 8):
        g_ = lax.rem(me_g + i, 8)
        arrived(hb.at[g_], R_G + g_)

    for z_ in range(4):
        term = jnp.dot(hb[...].reshape(8 * PAD, HID), dbuf[:, z_ * 128 : z_ * 128 + 128], preferred_element_type=F32)
        tf[z_] = term
        tb[z_] = term.astype(BF)
    for step in (1, -1, 2):
        x_ = lax.rem(x + step + 4, 4)
        send(tb.at[x_], r1b.at[x], R_1 + x, at_x(step))
    q_sum = tf[x]
    for step in (1, -1, 2):
        x_ = lax.rem(x + step + 4, 4)
        arrived(r1b.at[x_], R_1 + x_)
        q_sum = q_sum + r1b[x_].astype(F32)
    qs[...] = q_sum.reshape(8, PAD, 128)

    slot2 = zh * 4 + lax.rem(y, 2) * 2 + core
    side = y // 2
    for i in range(8):
        g_ = lax.rem(me_g + i, 8)
        target = dev(list_=zl * 8 + g_, tensor=x * 2 + side)
        cond = (zh != side) if i == 0 else None
        send(qs.at[g_, pl.ds(0, PASSES)], rb.at[slot2], R_2 + slot2, target, cond)

    @pl.when(zh == side)
    def _():
        rb[slot2] = qs[me_g, :PASSES, :]

    for s in range(8):
        own = (zh == s // 4) & (y == zh * 2 + (s % 4) // 2) & (core == s % 2)

        @pl.when(jnp.logical_not(own))
        def _():
            arrived(rb.at[s], R_2 + s)

    pooled = []
    squares = jnp.zeros((PASSES, 128), F32)
    for i in range(4):
        v = smean[:PASSES, i * 128 : i * 128 + 128] + rb[i] + rb[4 + i]
        squares = squares + v * v
        pooled.append(v)
    sb[ten] = jnp.broadcast_to(jnp.sum(squares, axis=1, keepdims=True), (PASSES, 128))
    for i in range(1, 8):
        t_ = lax.rem(ten + i, 8)
        send(sb.at[ten], sb.at[ten], R_3 + ten, dev(tensor=t_))
    for i in range(1, 8):
        t_ = lax.rem(ten + i, 8)
        arrived(sb.at[t_], R_3 + t_)
    total = sb[0]
    for t_ in range(1, 8):
        total = total + sb[t_]
    norm = lax.rsqrt(total / WIDTH + 1e-05)
    for i in range(4):
        cols = slice(i * 128, i * 128 + 128)
        e = pooled[i] * norm * og_in[:, cols]
        emb_out[:, cols] = e
        res_out[:, cols] = e - chosen_s[:PASSES, cols]

    for cp, cond in sends:
        if cond is None:
            cp.wait_send()
        else:
            pl.when(cond)(cp.wait_send)
    pl.loop(1, 32)(lambda i: req_copy(i).wait_send())
    pl.loop(1, 32)(lambda i: rsp_copy(i).wait_send())


def per_device(
    states, lengths, assign, norm_gain, gate_weight, up_weight, down_weight, out_gain, centroids
):
    any_ = pl.BlockSpec(memory_space=pl.ANY)
    smem = pl.BlockSpec(memory_space=pltpu.SMEM)
    vmem = pl.BlockSpec(memory_space=pltpu.VMEM)
    out = jax.ShapeDtypeStruct((PASSES, PART), F32)
    return pl.pallas_call(
        kernel,
        out_shape=(out, out),
        in_specs=[smem, smem] + [any_] * 7,
        out_specs=(vmem, vmem),
        scratch_shapes=[
            pltpu.VMEM((4, 1024, 2 * HID), BF),
            pltpu.VMEM((4, ROWS, 1024), BF),
            pltpu.VMEM((TILES, ROWS, 256), F32),
            pltpu.VMEM((OWN_ROWS, PART), BF),
            pltpu.VMEM((HID, 512), BF),
            pltpu.VMEM((ROWS, PART), BF),
            pltpu.VMEM((128, HID), BF),
            pltpu.VMEM((128, HID), BF),
            pltpu.VMEM((32, 128), F32),
            pltpu.VMEM((1, PART), F32),
            pltpu.VMEM((ROWS, 128), F32),
            pltpu.VMEM((PAD, ROWS), BF),
            pltpu.VMEM((PAD, 128), F32),
            pltpu.VMEM((8, PAD, HID), BF),
            pltpu.VMEM((4, 8 * PAD, 128), F32),
            pltpu.VMEM((4, 8 * PAD, 128), BF),
            pltpu.VMEM((4, 8 * PAD, 128), BF),
            pltpu.VMEM((8, PAD, 128), F32),
            pltpu.VMEM((8, PASSES, 128), F32),
            pltpu.VMEM((8, PASSES, 128), F32),
            pltpu.VMEM((32, 1, 128), jnp.int32),
            pltpu.VMEM((256, 128), jnp.int32),
            pltpu.VMEM((256, 512), F32),
            pltpu.VMEM((32, 8, 128), F32),
            pltpu.VMEM((32, 8, 128), F32),
            pltpu.VMEM((PAD, PART), F32),
            pltpu.VMEM((PAD, PART), F32),
            pltpu.SemaphoreType.DMA((N_SEND,)),
            pltpu.SemaphoreType.DMA((R_END,)),
            pltpu.SemaphoreType.DMA((12,)),
            pltpu.SemaphoreType.DMA((32,)),
            pltpu.SemaphoreType.DMA((32,)),
            pltpu.SemaphoreType.DMA((32,)),
            pltpu.SemaphoreType.DMA((32,)),
        ],
        compiler_params=pltpu.CompilerParams(has_side_effects=True, vmem_limit_bytes=56 << 20),
        name="passages",
    )(
        lengths,
        assign,
        states.reshape(ROWS, PART),
        norm_gain.reshape(32, 128),
        gate_weight,
        up_weight,
        down_weight,
        out_gain.reshape(1, PART),
        centroids,
    )


def solution(mesh):
    return jax.shard_map(
        per_device,
        mesh=mesh,
        in_specs=(
            P("list", None, "tensor"),
            P("list"),
            P("list"),
            P(),
            P("list", "tensor"),
            P("list", "tensor"),
            P("tensor", "list"),
            P("tensor"),
            P("list", "tensor"),
        ),
        out_specs=(P("list", "tensor"), P("list", "tensor")),
        check_vma=False,
    )
```

time: 559 us -> 155 us (0.28)
  waiting for transfers between devices: 455 us -> 0 us
  Pallas kernels: 0 us -> 150 us
  blocking collectives: 34.1 us -> 0 us
  matrix products: 26.1 us -> 0 us
  starting transfers between devices: 13.5 us -> 0 us
  between operations: 13.9 us -> 0.64 us
  other arithmetic: 6.25 us -> 0 us
    all_gather x4 -> x0, waiting for transfers between devices: 301 us -> none  [the longest x1 96.9 us: per_device(): whole = lax.all_gather(states, 'tensor', axis=2, tiled=True)]
    pallas_call x0 -> x1, Pallas kernels: none -> 150 us  [per_device(): pl.pallas_call(kernel, out_shape=(out, out), in_specs=[smem, smem] + [any...]
    reduce_scatter x1 -> x0, waiting for transfers between devices: 138 us -> none  [per_device(): mixed = lax.psum_scatter(terms, 'tensor', scatter_dimension=1, tiled=True)]
    dot_general x5 -> x0, matrix products: 26.1 us -> none  [the longest x1 14.9 us: per_device(): jnp.dot(hidden, lax.all_gather(down_weight, 'list', axis=1, tiled=True),...]
    psum x1 -> x0, blocking collectives: 22 us -> none  [per_device(): total = lax.psum(jnp.sum(pooled * pooled, axis=1), 'tensor')]
    all_to_all x2 -> x0, starting transfers between devices: 13.3 us -> none  [the longest x1 8.21 us: per_device(): lax.all_to_all(send_rows, 'list', split_axis=0, concat_axis=0, tiled=True)]
    all_to_all x2 -> x0, waiting for transfers between devices: 12.6 us -> none  [the longest x1 7.54 us: per_device(): lax.all_to_all(send_id, 'list', split_axis=0, concat_axis=0, tiled=True)]
    all_to_all x1 -> x0, blocking collectives: 12.1 us -> none  [per_device(): lax.all_to_all(differences, 'list', split_axis=0, concat_axis=0, tiled=True)]
  transfers between devices with their start and end apart: 7 -> 0, of which waited for: 7 -> 0; matrix products, arithmetic and copies ran while one was open for 3% -> 0% of each run, Pallas kernels for 0% -> 0%
where the time goes in v2:
time: 155 us; the launch traced here: 154 us
  Pallas kernels  150 us (97%)
  local copies, waits for them, and re-layouts  2.84 us (2%)
    pallas_call x1, Pallas kernels, per_device(): pl.pallas_call(kernel, out_shape=(out, out), in_specs=[smem, smem] + [any...  150 us

profile of v2, /device:TPU:6, one launch (start us, length us, event | category | flops | bytes accessed | tf_op | source)
XLA Modules:
  0.0 153.6 jit_solution(13197129671133529099)
XLA Ops:
  0.6 150.1 %passages.1 = (f32[24,512]{1,0:T(8,128)}, f32[24,512]{1,0:T(8,128)}) custom-call(s32[24]{0:T(128)} %lengths.1, s32[24]{0:T(128)} %assign.1, bf16[384,512]{1,0:T(8,128)(2,1)} %bitcast.3, f32[32,128]{1,0:T(8,128)} %bitcast.4, bf16[128,896]{1,0:T(8,128)(2,1)} %gate.1, bf16[128,896]{1,0:T(8,128)(2,1)} %up.1, bf16[896,128]{1,0:T(8,128)(2,1)} %down.1, ...), custom_call_target="tpu_custom_call" | custom-call | tf_op jit(solution)/shard_map/passages/pallas_call | solution.py:424
  150.8 1.4 copy.13
  152.2 1.4 copy.14

commit v3 on v2

--- a/solution.py
+++ b/solution.py
@@ -28,10 +28,11 @@
 R_CR = 44
 R_X = 46
 R_G = 62
-R_1 = 70
-R_2 = 74
-R_3 = 82
-R_END = 90
+R_1 = 66
+R_2 = 70
+R_3 = 74
+R_DS = 82
+R_END = 86
 N_SEND = 96
 
 
@@ -94,16 +95,60 @@
         cp.start()
         return cp
 
+    def dslot(z_, c_):
+        return dbuf.at[:, pl.ds(pl.multiple_of(z_ * 256 + c_ * 128, 128), 128)]
+
     def xslot(z_hi, half, x_):
         return xbuf.at[z_hi * 2 + half, :, pl.ds(pl.multiple_of(x_ * 256, 256), 256)]
 
+    def xslot(z_hi, half, x_):
+        return xbuf.at[z_hi * 2 + half, :, pl.ds(pl.multiple_of(x_ * 256, 256), 256)]
+
     cps_w = [local(gate, g_in), local(up, u_in), local(gain, gain_in)]
-    for half in range(2):
-        send(states.at[:, pl.ds(half * 256, 256)], xslot(zh, half, x), R_CR + half, partner)
+    cps_x = [local(states.at[:, pl.ds(half * 256, 256)], xslot(zh, half, x)) for half in range(2)]
+    cp_d = local(down, dslot(zl, core))
+    cp_s = local(states, sbuf)
+    cp_c = local(centroids, cbuf)
+    cp_o = local(out_gain, og_in)
+    barrier = pltpu.get_barrier_semaphore()
+
+    def greet_list(i):
+        pl.semaphore_signal(barrier, inc=1, device_id=dev(list_=lax.rem(lst + i, 32)), device_id_type=MESH)
+
+    def greet_tensor(i):
+        pl.semaphore_signal(barrier, inc=1, device_id=dev(tensor=lax.rem(ten + i, 8)), device_id_type=MESH)
+
+    def greet_across(i):
+        there = dev(list_=zl * 8 + lax.rem(y + i, 4) * 2 + core, tensor=x * 2 + 1 - zh)
+        pl.semaphore_signal(barrier, inc=1, device_id=there, device_id_type=MESH)
+
+    pl.loop(1, 32)(greet_list)
+    pl.loop(1, 8)(greet_tensor)
+    pl.loop(1, 4)(greet_across)
+    pl.semaphore_wait(barrier, 31 + 7 + 3)
     for step in (1, -1, 2):
         for half in range(2):
             send(states.at[:, pl.ds(half * 256, 256)], xslot(zh, half, x), R_X + x * 2 + half, at_x(step))
-    cps_x = [local(states.at[:, pl.ds(half * 256, 256)], xslot(zh, half, x)) for half in range(2)]
+
+    def cross(n):
+        half = lax.rem(y + n, 2)
+        send(states.at[:, pl.ds(pl.multiple_of(half * 256, 256), 256)], xslot(zh, half, x), R_CR + n, partner)
+
+    def crossed(n):
+        half = lax.rem(y + n, 2)
+        block = xslot(1 - zh, half, x)
+        arrived(block, R_CR + n)
+        for step in (1, -1, 2):
+            send(block, block, R_X + 8 + x * 2 + n, at_x(step))
+
+    def x_arrived(n):
+        for step in (1, -1, 2):
+            x_ = lax.rem(x + step + 4, 4)
+            if n is None:
+                for half in range(2):
+                    arrived(xslot(zh, half, x_), R_X + x_ * 2 + half)
+            else:
+                arrived(xslot(1 - zh, lax.rem(y + n, 2), x_), R_X + 8 + x_ * 2 + n)
 
     for cp in cps_w:
         cp.wait()
@@ -156,26 +201,37 @@
             arrived(part, R_H + d * 4 + k)
             send(part, part, R_SH + d * 4 + k, sibling)
 
-    def dslot(z_):
-        return dbuf.at[:, pl.ds(pl.multiple_of(z_ * 128, 128), 128)]
-
     def down_column(k):
         z_ = place(k)
+        block = dslot(z_, core)
         if k == 0:
-            send(down, dslot(z_), R_DN + z_, at_z(lax.rem(zl + 1, 4)), zl < 3)
-            send(down, dslot(z_), R_DN + z_, at_z(lax.rem(zl + 3, 4)), zl > 0)
+            cp_d.wait()
+            send(block, block, R_DN + z_, at_z(lax.rem(zl + 1, 4)), zl < 3)
+            send(block, block, R_DN + z_, at_z(lax.rem(zl + 3, 4)), zl > 0)
         else:
-            arrived(dslot(z_), R_DN + z_)
+            arrived(block, R_DN + z_)
             onward = jnp.where(z_ < zl, zl + 1, zl - 1)
             there = (onward >= 0) & (onward < 4)
-            send(dslot(z_), dslot(z_), R_DN + z_, at_z(lax.rem(onward + 4, 4)), there)
+            send(block, block, R_DN + z_, at_z(lax.rem(onward + 4, 4)), there)
+        send(block, block, R_DS + k, sibling)
+
+    def product(yy, k):
+        ks = pl.ds(pl.multiple_of(place(k) * 256, 256), 256)
+        for j in range(TILES):
+            acc[j] += jnp.dot(xbuf[yy, :, ks], wbuf[yy, ks, j * 256 : j * 256 + 256], preferred_element_type=F32)
+
+    def from_sibling_column(k):
+        arrived(wblock(y, place(k), 1 - core), R_SC + k)
+
+    def from_sibling_neighbour(d, k):
+        arrived(wblock(y_of(2 * d - 1), place(k), 1 - core), R_SY + d * 4 + k)
+
+    def from_sibling_halves(k):
+        for d in range(2):
+            arrived(wblock(y_of(2), place(k), 1 - core, d * 64, 64), R_SH + d * 4 + k)
 
     column(0)
 
-    cp_d = local(down, dslot(zl))
-    cp_s = local(states, sbuf)
-    cp_c = local(centroids, cbuf)
-    cp_o = local(out_gain, og_in)
     lane = lax.broadcasted_iota(jnp.int32, (1, 128), 1)
     arow = jnp.full((1, 128), -1, jnp.int32)
     sub = lax.broadcasted_iota(jnp.int32, (PAD, 128), 0)
@@ -206,6 +262,7 @@
     smean[...] = jnp.dot(mask_s[...], sbuf[...], preferred_element_type=F32) * inv_s[:, :1]
 
     column(1)
+    cross(0)
     neighbour(0)
 
     def req_from(i):
@@ -252,28 +309,41 @@
     pl.loop(1, 32)(lambda i: rsp_copy(i).start())
 
     column(2)
+    cross(1)
     neighbour(1)
-    down_column(0)
-    column(3)
-
-    for half in range(2):
-        arrived(xslot(1 - zh, half, x), R_CR + half)
-        for step in (1, -1, 2):
-            send(xslot(1 - zh, half, x), xslot(1 - zh, half, x), R_X + 8 + x * 2 + half, at_x(step))
-
-    neighbour(2)
-    down_column(1)
-    neighbour(3)
-    down_column(2)
-
+    halves(0)
+    crossed(0)
+    acc[...] = jnp.zeros_like(acc)
     for cp in cps_x:
         cp.wait()
-    for crossed, z_hi in ((0, zh), (1, 1 - zh)):
-        for step in (1, -1, 2):
-            x_ = lax.rem(x + step + 4, 4)
-            for half in range(2):
-                arrived(xslot(z_hi, half, x_), R_X + crossed * 8 + x_ * 2 + half)
-
+    x_arrived(None)
+    x_arrived(0)
+    for k in range(3):
+        from_sibling_column(k)
+        product(y, k)
+    column(3)
+    down_column(0)
+    crossed(1)
+    from_sibling_column(3)
+    product(y, 3)
+    neighbour(2)
+    y_a = jnp.where(y // 2 == zh, y + 1 - 2 * lax.rem(y, 2), lax.rem(y + 3 - 2 * lax.rem(y, 2), 4))
+    y_b = lax.rem(y_a + 2, 4)
+    for k in range(3):
+        for d in range(2):
+            from_sibling_neighbour(d, k)
+        product(y_a, k)
+    for k in (1, 2):
+        halves(k)
+    for k in range(3):
+        from_sibling_halves(k)
+        product(y_of(2), k)
+    neighbour(3)
+    down_column(1)
+    for d in range(2):
+        from_sibling_neighbour(d, 3)
+    product(y_a, 3)
+    x_arrived(1)
     @pl.loop(0, ROWS // 32)
     def _(r):
         rows = pl.ds(pl.multiple_of(r * 32, 32), 32)
@@ -285,34 +355,11 @@
         mean = jnp.sum(total, axis=1, keepdims=True) / WIDTH
         scale_s[rows, :] = jnp.broadcast_to(lax.rsqrt(mean + 1e-05), (32, 128))
 
-    def product(yy, start, depth, init):
-        @pl.loop(0, TILES)
-        def _(j):
-            cols = pl.ds(pl.multiple_of(j * 256, 256), 256)
-            ks = pl.ds(start, depth)
-            r = jnp.dot(xbuf[yy, :, ks], wbuf[yy, ks, cols], preferred_element_type=F32)
-            if init:
-                acc[j] = r
-            else:
-                acc[j] += r
-
     for k in range(4):
-        arrived(wblock(y, place(k), 1 - core), R_SC + k)
-    product(y, 0, 1024, True)
-    for d, step in ((0, -1), (1, 1)):
-        for k in range(4):
-            arrived(wblock(y_of(step), place(k), 1 - core), R_SY + d * 4 + k)
-        product(y_of(step), 0, 1024, False)
-    for k in range(4):
-        halves(k)
-        for d in range(2):
-            arrived(wblock(y_of(2), place(k), 1 - core, d * 64, 64), R_SH + d * 4 + k)
-        if k < 3:
-            product(y_of(2), pl.multiple_of(place(k) * 256, 256), 256, False)
-    down_column(3)
-    cp_d.wait()
-    cp_o.wait()
-
+        product(y_b, k)
+    down_column(2)
+    halves(3)
+    from_sibling_halves(3)
     yy = y_of(2)
     ks = pl.ds(pl.multiple_of(place(3) * 256, 256), 256)
     for j in range(TILES):
@@ -321,11 +368,14 @@
         u = r[:, 128:] * scale_s[...]
         h = (g / (1.0 + jnp.exp(-g)) * u).astype(BF)
         pooled_h = jnp.dot(mask_s[...], h, preferred_element_type=F32) * inv_s[...]
-        hb[me_g, :, j * 128 : j * 128 + 128] = pooled_h.astype(BF)
-
-    for i in range(1, 8):
-        g_ = lax.rem(me_g + i, 8)
-        send(hb.at[me_g], hb.at[me_g], R_G + me_g, dev(list_=zl * 8 + g_))
+        hb[y, :, j * 128 : j * 128 + 128] = pooled_h.astype(BF)
+
+    for step in (1, -1, 2):
+        send(hb.at[y], hb.at[y], R_G + y, at_y(step))
+    down_column(3)
+    for k in range(4):
+        arrived(dslot(place(k), 1 - core), R_DS + k)
+    cp_o.wait()
 
     def rsp_from(i):
         peer = lax.rem(lst + i, 32)
@@ -345,12 +395,12 @@
         one = jnp.where(wide == own_col[:, :1] * 8 + q * 2 + slot, 1.0, 0.0).astype(BF)
         chosen_s[:, q * 128 : q * 128 + 128] = jnp.dot(one, table, preferred_element_type=F32)
 
-    for i in range(1, 8):
-        g_ = lax.rem(me_g + i, 8)
-        arrived(hb.at[g_], R_G + g_)
+    for step in (1, -1, 2):
+        y_ = y_of(step)
+        arrived(hb.at[y_], R_G + y_)
 
     for z_ in range(4):
-        term = jnp.dot(hb[...].reshape(8 * PAD, HID), dbuf[:, z_ * 128 : z_ * 128 + 128], preferred_element_type=F32)
+        term = jnp.dot(hb[...].reshape(4 * PAD, HID), dbuf[:, z_ * 256 : z_ * 256 + 256], preferred_element_type=F32)
         tf[z_] = term
         tb[z_] = term.astype(BF)
     for step in (1, -1, 2):
@@ -361,31 +411,31 @@
         x_ = lax.rem(x + step + 4, 4)
         arrived(r1b.at[x_], R_1 + x_)
         q_sum = q_sum + r1b[x_].astype(F32)
-    qs[...] = q_sum.reshape(8, PAD, 128)
-
-    slot2 = zh * 4 + lax.rem(y, 2) * 2 + core
+    qs[...] = q_sum.reshape(4, PAD, 256)
+    slot2 = zh * 2 + lax.rem(y, 2)
     side = y // 2
-    for i in range(8):
-        g_ = lax.rem(me_g + i, 8)
-        target = dev(list_=zl * 8 + g_, tensor=x * 2 + side)
-        cond = (zh != side) if i == 0 else None
-        send(qs.at[g_, pl.ds(0, PASSES)], rb.at[slot2], R_2 + slot2, target, cond)
+    for step in (0, 1, -1, 2):
+        y_ = y_of(step)
+        target = dev(list_=zl * 8 + y_ * 2 + core, tensor=x * 2 + side)
+        cond = (zh != side) if step == 0 else None
+        send(qs.at[y_, pl.ds(0, PASSES)], rb.at[slot2], R_2 + slot2, target, cond)
 
     @pl.when(zh == side)
     def _():
-        rb[slot2] = qs[me_g, :PASSES, :]
-
-    for s in range(8):
-        own = (zh == s // 4) & (y == zh * 2 + (s % 4) // 2) & (core == s % 2)
+        rb[slot2] = qs[y, :PASSES, :]
+
+    for n in range(4):
+        own = (zh == n // 2) & (y == zh * 2 + n % 2)
 
         @pl.when(jnp.logical_not(own))
         def _():
-            arrived(rb.at[s], R_2 + s)
+            arrived(rb.at[n], R_2 + n)
 
     pooled = []
     squares = jnp.zeros((PASSES, 128), F32)
     for i in range(4):
-        v = smean[:PASSES, i * 128 : i * 128 + 128] + rb[i] + rb[4 + i]
+        half = slice(i % 2 * 128, i % 2 * 128 + 128)
+        v = smean[:PASSES, i * 128 : i * 128 + 128] + rb[i // 2, :, half] + rb[2 + i // 2, :, half]
         squares = squares + v * v
         pooled.append(v)
     sb[ten] = jnp.broadcast_to(jnp.sum(squares, axis=1, keepdims=True), (PASSES, 128))
@@ -431,7 +481,7 @@
             pltpu.VMEM((4, ROWS, 1024), BF),
             pltpu.VMEM((TILES, ROWS, 256), F32),
             pltpu.VMEM((OWN_ROWS, PART), BF),
-            pltpu.VMEM((HID, 512), BF),
+            pltpu.VMEM((HID, 1024), BF),
             pltpu.VMEM((ROWS, PART), BF),
             pltpu.VMEM((128, HID), BF),
             pltpu.VMEM((128, HID), BF),
@@ -440,12 +490,12 @@
             pltpu.VMEM((ROWS, 128), F32),
             pltpu.VMEM((PAD, ROWS), BF),
             pltpu.VMEM((PAD, 128), F32),
-            pltpu.VMEM((8, PAD, HID), BF),
-            pltpu.VMEM((4, 8 * PAD, 128), F32),
-            pltpu.VMEM((4, 8 * PAD, 128), BF),
-            pltpu.VMEM((4, 8 * PAD, 128), BF),
-            pltpu.VMEM((8, PAD, 128), F32),
-            pltpu.VMEM((8, PASSES, 128), F32),
+            pltpu.VMEM((4, PAD, HID), BF),
+            pltpu.VMEM((4, 4 * PAD, 256), F32),
+            pltpu.VMEM((4, 4 * PAD, 256), BF),
+            pltpu.VMEM((4, 4 * PAD, 256), BF),
+            pltpu.VMEM((4, PAD, 256), F32),
+            pltpu.VMEM((4, PASSES, 256), F32),
             pltpu.VMEM((8, PASSES, 128), F32),
             pltpu.VMEM((32, 1, 128), jnp.int32),
             pltpu.VMEM((256, 128), jnp.int32),
@@ -462,7 +512,7 @@
             pltpu.SemaphoreType.DMA((32,)),
             pltpu.SemaphoreType.DMA((32,)),
         ],
-        compiler_params=pltpu.CompilerParams(has_side_effects=True, vmem_limit_bytes=56 << 20),
+        compiler_params=pltpu.CompilerParams(collective_id=0, has_side_effects=True, vmem_limit_bytes=56 << 20),
         name="passages",
     )(
         lengths,

time: 155 us -> 124 us (0.80)
  Pallas kernels: 150 us -> 120 us
    pallas_call x1, Pallas kernels: 150 us -> 120 us  [per_device(): pl.pallas_call(kernel, out_shape=(out, out), in_specs=[smem, smem] + [any...]
where the time goes in v3:
time: 124 us
  Pallas kernels  120 us (97%)
  local copies, waits for them, and re-layouts  2.84 us (2%)
    pallas_call x1, Pallas kernels, per_device(): pl.pallas_call(kernel, out_shape=(out, out), in_specs=[smem, smem] + [any...  120 us
    unnamed x2, local copies, waits for them, and re-layouts  2.84 us

profile of v3, /device:TPU:6, one launch (start us, length us, event | category | flops | bytes accessed | tf_op | source)
XLA Modules:
  0.0 123.7 jit_solution(11220093698692715896)
XLA Ops:
  0.6 120.2 %passages.1 = (f32[24,512]{1,0:T(8,128)}, f32[24,512]{1,0:T(8,128)}) custom-call(s32[24]{0:T(128)} %lengths.1, s32[24]{0:T(128)} %assign.1, bf16[384,512]{1,0:T(8,128)(2,1)} %bitcast.3, f32[32,128]{1,0:T(8,128)} %bitcast.4, bf16[128,896]{1,0:T(8,128)(2,1)} %gate.1, bf16[128,896]{1,0:T(8,128)(2,1)} %up.1, bf16[896,128]{1,0:T(8,128)(2,1)} %down.1, ...), custom_call_target="tpu_custom_call" | custom-call | tf_op jit(solution)/shard_map/passages/pallas_call | solution.py:474
  120.8 1.4 %copy.13 = f32[24,512]{1,0:T(8,128)} copy(f32[24,512]{1,0:T(8,128)} %get-tuple-element.4) | data formatting | bytes 98304
  122.2 1.4 %copy.14 = f32[24,512]{1,0:T(8,128)} copy(f32[24,512]{1,0:T(8,128)} %get-tuple-element.5) | data formatting | bytes 98304

commit v4 on v3

v4 whole, which is shorter than its diff:
```python
import functools

import jax
import jax.numpy as jnp
from jax import lax
from jax.experimental import pallas as pl
from jax.experimental.pallas import tpu as pltpu
from jax.sharding import PartitionSpec as P

MESH = pl.DeviceIdType.MESH
BF = jnp.bfloat16
F32 = jnp.float32

PASSES, SEQ, PART, WIDTH = 24, 16, 512, 4096
ROWS = PASSES * SEQ
HID = 896
TILES = HID // 128
PAD = 32
OWN_ROWS = 4096

R_Z = 0
R_Y = 4
R_H = 12
R_SC = 16
R_SY = 20
R_SH = 24
R_DN = 28
R_DS = 32
R_CR = 33
R_X = 35
R_G = 39
R_1 = 40
R_2 = 41
R_3 = 42
R_REQ = 43
R_RSP = 44
R_END = 45
S_W, S_Z, S_X, S_CR, S_DZ, S_DS, S_G, S_1, S_2, S_3, S_REQ, S_RSP, S_END = range(13)


def kernel(
    lengths, assign, states, gain, gate, up, down, out_gain, centroids,
    out,
    wbuf, xbuf, acc, cbuf, dbuf, sbuf, g_in, u_in, gain_in, og_in,
    scale_s, mask_s, inv_s, hb, tf, tb, r1b, qs, rb, sb, abuf, pick, cacc, resp, gotc, chosen_s, smean, out_s,
    ss, rs, ls,
):
    lst = lax.axis_index("list")
    ten = lax.axis_index("tensor")
    core = lax.rem(lst, 2)
    y = lax.rem(lst // 2, 4)
    zl = lst // 8
    x = ten // 2
    zh = lax.rem(ten, 2)
    me_g = lax.rem(lst, 8)

    def dev(list_=None, tensor=None):
        return {"list": lst if list_ is None else list_, "tensor": ten if tensor is None else tensor}

    def at_z(z):
        return dev(list_=z * 8 + me_g)

    def at_y(step):
        return dev(list_=zl * 8 + lax.rem(y + step + 4, 4) * 2 + core)

    def at_x(step):
        return dev(tensor=lax.rem(x + step + 4, 4) * 2 + zh)

    sibling = dev(list_=lst + 1 - 2 * core)
    partner = dev(tensor=x * 2 + 1 - zh)

    def remote(src, dst, kind, recv, device):
        return pltpu.make_async_remote_copy(
            src_ref=src, dst_ref=dst, send_sem=ss.at[kind], recv_sem=rs.at[recv],
            device_id=device, device_id_type=MESH,
        )

    def send(src, dst, kind, recv, device, cond=None):
        cp = remote(src, dst, kind, recv, device)
        if cond is None:
            cp.start()
        else:
            pl.when(cond)(cp.start)

    def arrived(dst, recv):
        remote(dst, dst, 0, recv, sibling).wait_recv()

    def sent(src, kind):
        remote(src, src, kind, 0, sibling).wait_send()

    locals_ = []

    def local(src, dst):
        cp = pltpu.make_async_copy(src, dst, ls.at[len(locals_)])
        locals_.append(cp)
        cp.start()
        return cp

    def dslot(z_, c_):
        return dbuf.at[:, pl.ds(pl.multiple_of(z_ * 256 + c_ * 128, 128), 128)]

    def xslot(z_hi, half, x_):
        return xbuf.at[z_hi * 2 + half, :, pl.ds(pl.multiple_of(x_ * 256, 256), 256)]

    def xslot(z_hi, half, x_):
        return xbuf.at[z_hi * 2 + half, :, pl.ds(pl.multiple_of(x_ * 256, 256), 256)]

    cps_w = [local(gate, g_in), local(up, u_in), local(gain, gain_in)]
    cps_x = [local(states.at[:, pl.ds(half * 256, 256)], xslot(zh, half, x)) for half in range(2)]
    cp_d = local(down, dslot(zl, core))
    cp_s = local(states, sbuf)
    cp_c = local(centroids, cbuf)
    cp_o = local(out_gain, og_in)
    barrier = pltpu.get_barrier_semaphore()

    def greet_list(i):
        pl.semaphore_signal(barrier, inc=1, device_id=dev(list_=lax.rem(lst + i, 32)), device_id_type=MESH)

    def greet_tensor(i):
        pl.semaphore_signal(barrier, inc=1, device_id=dev(tensor=lax.rem(ten + i, 8)), device_id_type=MESH)

    def greet_across(i):
        there = dev(list_=zl * 8 + lax.rem(y + i, 4) * 2 + core, tensor=x * 2 + 1 - zh)
        pl.semaphore_signal(barrier, inc=1, device_id=there, device_id_type=MESH)

    pl.loop(1, 32)(greet_list)
    pl.loop(1, 8)(greet_tensor)
    pl.loop(1, 4)(greet_across)
    for cp in cps_w:
        cp.wait()
    eye = lax.broadcasted_iota(jnp.int32, (128, 128), 0) == lax.broadcasted_iota(jnp.int32, (128, 128), 1)
    gcol = jnp.sum(jnp.where(eye, gain_in[pl.ds(lst, 1), :], 0.0), axis=1, keepdims=True)
    own_rows = pl.ds(pl.multiple_of(y * 1024 + zl * 256 + core * 128, 128), 128)
    for j in range(TILES):
        wbuf[own_rows, j * 256 : j * 256 + 128] = (g_in[:, j * 128 : j * 128 + 128].astype(F32) * gcol).astype(BF)
        wbuf[own_rows, j * 256 + 128 : j * 256 + 256] = (u_in[:, j * 128 : j * 128 + 128].astype(F32) * gcol).astype(BF)

    pl.semaphore_wait(barrier, 31 + 7 + 3)
    for step in (1, -1, 2):
        for half in range(2):
            send(states.at[:, pl.ds(half * 256, 256)], xslot(zh, half, x), S_X, R_X + half, at_x(step))

    def cross(n):
        half = lax.rem(y + n, 2)
        send(states.at[:, pl.ds(pl.multiple_of(half * 256, 256), 256)], xslot(zh, half, x), S_CR, R_CR + n, partner)

    def crossed(n):
        half = lax.rem(y + n, 2)
        block = xslot(1 - zh, half, x)
        arrived(block, R_CR + n)
        for step in (1, -1, 2):
            send(block, block, S_X, R_X + 2 + n, at_x(step))

    def x_arrived(n):
        arrived(xbuf.at[0, :, pl.ds(0, 768)], R_X + n)

    def wblock(y_, z_, c_, start=0, rows=128):
        return wbuf.at[pl.ds(pl.multiple_of(y_ * 1024 + z_ * 256 + c_ * 128 + start, 64), rows)]

    def place(k):
        inner = (zl == 1) | (zl == 2)
        o = jnp.where(inner, 1 - k, k) if k < 2 else k
        return jnp.where(zl < 2, o, 3 - o)

    inner_z = (zl == 1) | (zl == 2)

    def y_of(step):
        return lax.rem(y + step + 4, 4)

    def column(k):
        z_ = place(k)
        block = wblock(y, z_, core)
        if k == 0:
            send(block, block, S_Z, R_Z + z_, at_z(lax.rem(zl + 1, 4)), zl < 3)
            send(block, block, S_Z, R_Z + z_, at_z(lax.rem(zl + 3, 4)), zl > 0)
        else:
            arrived(block, R_Z + z_)
            onward = jnp.where(z_ < zl, zl + 1, zl - 1)
            send(block, block, S_Z, R_Z + z_, at_z(lax.rem(onward + 4, 4)), inner_z)
        send(block, block, S_W, R_Y + k, at_y(1))
        send(block, block, S_W, R_Y + 4 + k, at_y(-1))
        send(block, block, S_W, R_SC + k, sibling)

    def neighbour(k):
        z_ = place(k)
        for d, step in ((0, -1), (1, 1)):
            block = wblock(y_of(step), z_, core)
            arrived(block, R_Y + d * 4 + k)
            part = wblock(y_of(step), z_, core, d * 64, 64)
            send(part, part, S_W, R_H + k, at_y(-step))
            send(block, block, S_W, R_SY + k, sibling)

    def halves(k):
        block = wblock(y_of(2), place(k), core)
        arrived(block, R_H + k)
        send(block, block, S_W, R_SH + k, sibling)

    def down_column(k):
        z_ = place(k)
        block = dslot(z_, core)
        if k == 0:
            cp_d.wait()
            send(block, block, S_DZ, R_DN + z_, at_z(lax.rem(zl + 1, 4)), zl < 3)
            send(block, block, S_DZ, R_DN + z_, at_z(lax.rem(zl + 3, 4)), zl > 0)
        else:
            arrived(block, R_DN + z_)
            onward = jnp.where(z_ < zl, zl + 1, zl - 1)
            send(block, block, S_DZ, R_DN + z_, at_z(lax.rem(onward + 4, 4)), inner_z)
        send(block, block, S_DS, R_DS, sibling)

    def product(yy, k):
        ks = pl.ds(pl.multiple_of(place(k) * 256, 256), 256)
        rows = pl.ds(pl.multiple_of(yy * 1024 + place(k) * 256, 256), 256)
        for j in range(TILES):
            acc[j] += jnp.dot(xbuf[yy, :, ks], wbuf[rows, j * 256 : j * 256 + 256], preferred_element_type=F32)

    def squares_of(yy, init):
        @pl.loop(0, ROWS // 32)
        def _(r):
            rows = pl.ds(pl.multiple_of(r * 32, 32), 32)
            total = jnp.zeros((32, 128), F32) if init else scale_s[rows, :]
            for c in range(8):
                v = xbuf[yy, rows, c * 128 : c * 128 + 128].astype(F32)
                total = total + v * v
            scale_s[rows, :] = total

    def from_sibling_column(k):
        arrived(wblock(y, place(k), 1 - core), R_SC + k)

    def from_sibling_neighbours(k):
        arrived(wbuf.at[pl.ds(0, 256)], R_SY + k)

    def from_sibling_halves(k):
        arrived(wblock(y_of(2), place(k), 1 - core), R_SH + k)

    column(0)

    lane = lax.broadcasted_iota(jnp.int32, (1, 128), 1)
    arow = jnp.full((1, 128), -1, jnp.int32)
    sub = lax.broadcasted_iota(jnp.int32, (PAD, 128), 0)
    acol = jnp.full((PAD, 128), -1, jnp.int32)
    lcol = jnp.ones((PAD, 128), jnp.int32)
    for p in range(PASSES):
        arow = jnp.where(lane == p, assign[p], arow)
        acol = jnp.where(sub == p, assign[p], acol)
        lcol = jnp.where(sub == p, lengths[p], lcol)
    abuf[lst] = arow

    @pl.loop(1, 32)
    def _(i):
        peer = lax.rem(lst + i, 32)
        send(abuf.at[lst], abuf.at[lst], S_REQ, R_REQ, dev(list_=peer))

    slot_row = lax.broadcasted_iota(jnp.int32, (PAD, ROWS), 0)
    slot_col = lax.broadcasted_iota(jnp.int32, (PAD, ROWS), 1)
    length = lcol[:, :1]
    in_pass = (slot_col >= slot_row * SEQ) & (slot_col < slot_row * SEQ + length) & (slot_row < PASSES)
    mask_s[...] = jnp.where(in_pass, 1.0, 0.0).astype(BF)
    inv_s[...] = 1.0 / lcol.astype(F32)
    cp_s.wait()
    smean[...] = jnp.dot(mask_s[...], sbuf[...], preferred_element_type=F32) * inv_s[:, :1]

    column(1)
    cross(0)
    pl.when(inner_z)(lambda: column(2))
    neighbour(0)

    arrived(abuf.at[pl.ds(0, 31)], R_REQ)
    cp_c.wait()
    wanted = jnp.broadcast_to(abuf[...], (32, 8, 128))
    lanes3 = lax.broadcasted_iota(jnp.int32, (32, 8, 128), 2)
    odd3 = lax.rem(lax.broadcasted_iota(jnp.int32, (32, 8, 128), 1), 2) == 1
    mine = (wanted >= lst * OWN_ROWS) & (wanted < lst * OWN_ROWS + OWN_ROWS)
    first = jnp.min(jnp.where(mine, lanes3, 128), axis=2, keepdims=True)
    last = jnp.max(jnp.where(mine, lanes3, -1), axis=2, keepdims=True)
    chosen_lane = jnp.where(odd3, last, first)
    hit = mine & (lanes3 == chosen_lane)
    ids = jnp.sum(jnp.where(hit, wanted - lst * OWN_ROWS, 0), axis=2, keepdims=True)
    pick[...] = jnp.broadcast_to(ids, (32, 8, 128)).reshape(256, 128)
    cacc[...] = jnp.zeros_like(cacc)

    @pl.loop(0, 8)
    def _(kc):
        base = lax.broadcasted_iota(jnp.int32, (256, 512), 1) + kc * 512
        one = jnp.where(base == pick[:, :1], 1.0, 0.0).astype(BF)
        cacc[...] += jnp.dot(one, cbuf[pl.ds(pl.multiple_of(kc * 512, 512), 512), :], preferred_element_type=F32)

    quarter = lax.rem(lax.broadcasted_iota(jnp.int32, (256, 128), 0), 8) // 2
    out_rows = jnp.zeros((256, 128), F32)
    for q in range(4):
        out_rows = jnp.where(quarter == q, cacc[:, q * 128 : q * 128 + 128], out_rows)
    resp[...] = out_rows.reshape(32, 8, 128)
    gotc[lst] = resp[lst]

    @pl.loop(1, 32)
    def _(i):
        peer = lax.rem(lst + i, 32)
        send(resp.at[peer], gotc.at[lst], S_RSP, R_RSP, dev(list_=peer))

    outer_z = jnp.logical_not(inner_z)
    pl.when(inner_z)(lambda: column(3))
    neighbour(1)
    pl.when(outer_z)(lambda: column(2))
    cross(1)
    for cp in cps_x:
        cp.wait()
    for half in range(2):
        x_arrived(half)
    acc[...] = jnp.zeros_like(acc)
    squares_of(zh * 2, True)
    squares_of(zh * 2 + 1, False)
    halves(0)
    crossed(0)
    y_a = jnp.where(y // 2 == zh, y + 1 - 2 * lax.rem(y, 2), lax.rem(y + 3 - 2 * lax.rem(y, 2), 4))
    y_b = lax.rem(y_a + 2, 4)
    for k in range(2):
        from_sibling_neighbours(k)
        product(y_a, k)
    neighbour(2)
    pl.when(jnp.logical_not(inner_z))(lambda: column(3))
    crossed(1)
    down_column(0)
    halves(1)
    from_sibling_neighbours(2)
    product(y_a, 2)
    x_arrived(2)
    for k in range(4):
        from_sibling_column(k)
        product(y, k)
    squares_of((1 - zh) * 2 + lax.rem(y, 2), False)
    neighbour(3)
    halves(2)
    down_column(1)
    pl.when(inner_z)(lambda: down_column(2))
    for k in range(3):
        from_sibling_halves(k)
        product(y_of(2), k)
    from_sibling_neighbours(3)
    product(y_a, 3)
    x_arrived(3)
    squares_of((1 - zh) * 2 + lax.rem(y + 1, 2), False)
    for k in range(4):
        product(y_b, k)
    scale_s[...] = jnp.broadcast_to(
        lax.rsqrt(jnp.sum(scale_s[...], axis=1, keepdims=True) / WIDTH + 1e-05), (ROWS, 128)
    )
    halves(3)
    pl.when(inner_z)(lambda: down_column(3))
    from_sibling_halves(3)
    yy = y_of(2)
    ks = pl.ds(pl.multiple_of(place(3) * 256, 256), 256)
    wrows = pl.ds(pl.multiple_of(yy * 1024 + place(3) * 256, 256), 256)
    for j in range(TILES):
        r = acc[j] + jnp.dot(xbuf[yy, :, ks], wbuf[wrows, j * 256 : j * 256 + 256], preferred_element_type=F32)
        g = r[:, :128] * scale_s[...]
        u = r[:, 128:] * scale_s[...]
        h = (g / (1.0 + jnp.exp(-g)) * u).astype(BF)
        pooled_h = jnp.dot(mask_s[...], h, preferred_element_type=F32) * inv_s[...]
        hb[y, :, j * 128 : j * 128 + 128] = pooled_h.astype(BF)

    for step in (1, -1, 2):
        send(hb.at[y], hb.at[y], S_G, R_G, at_y(step))
    @pl.when(jnp.logical_not(inner_z))
    def _():
        down_column(2)
        down_column(3)

    arrived(dbuf.at[:, pl.ds(0, 512)], R_DS)
    cp_o.wait()

    arrived(gotc.at[pl.ds(0, 31)], R_RSP)
    own_col = acol >> 12
    own_row = jnp.where(lane < PASSES, arow >> 12, -1)
    before = (own_col == own_row) & (lax.broadcasted_iota(jnp.int32, (PAD, 128), 1) < sub)
    slot = jnp.max(jnp.where(before, 1, 0), axis=1, keepdims=True)
    wide = lax.broadcasted_iota(jnp.int32, (PAD, 256), 1)
    table = gotc[...].reshape(256, 128).astype(BF)
    for q in range(4):
        one = jnp.where(wide == own_col[:, :1] * 8 + q * 2 + slot, 1.0, 0.0).astype(BF)
        chosen_s[:, q * 128 : q * 128 + 128] = jnp.dot(one, table, preferred_element_type=F32)

    arrived(hb.at[pl.ds(0, 3)], R_G)

    for z_ in range(4):
        term = jnp.dot(hb[...].reshape(4 * PAD, HID), dbuf[:, z_ * 256 : z_ * 256 + 256], preferred_element_type=F32)
        term = jnp.concatenate([term[g * PAD : g * PAD + PASSES] for g in range(4)], axis=0)
        tf[z_] = term
        tb[z_] = term.astype(BF)
    for step in (1, -1, 2):
        x_ = lax.rem(x + step + 4, 4)
        send(tb.at[x_], r1b.at[x], S_1, R_1, at_x(step))
    arrived(r1b.at[pl.ds(0, 3)], R_1)
    q_sum = tf[x]
    for step in (1, -1, 2):
        x_ = lax.rem(x + step + 4, 4)
        q_sum = q_sum + r1b[x_].astype(F32)
    qs[...] = q_sum.reshape(4, PASSES, 256)
    slot2 = zh * 2 + lax.rem(y, 2)
    side = y // 2
    for step in (0, 1, -1, 2):
        y_ = y_of(step)
        target = dev(list_=zl * 8 + y_ * 2 + core, tensor=x * 2 + side)
        cond = (zh != side) if step == 0 else None
        send(qs.at[y_], rb.at[slot2], S_2, R_2, target, cond)

    @pl.when(zh == side)
    def _():
        rb[slot2] = qs[y]

    @pl.when(zh == side)
    def _():
        arrived(rb.at[pl.ds(0, 3)], R_2)

    @pl.when(zh != side)
    def _():
        arrived(rb, R_2)

    pooled = []
    squares = jnp.zeros((PASSES, 128), F32)
    for i in range(4):
        half = slice(i % 2 * 128, i % 2 * 128 + 128)
        v = smean[:PASSES, i * 128 : i * 128 + 128] + rb[i // 2, :, half] + rb[2 + i // 2, :, half]
        squares = squares + v * v
        pooled.append(v)
    turn = lax.broadcasted_iota(jnp.int32, (PASSES, 128), 0) == lax.broadcasted_iota(jnp.int32, (PASSES, 128), 1)
    sb[ten] = jnp.sum(jnp.where(turn, jnp.sum(squares, axis=1, keepdims=True), 0.0), axis=0, keepdims=True)
    for i in range(1, 8):
        t_ = lax.rem(ten + i, 8)
        send(sb.at[ten], sb.at[ten], S_3, R_3, dev(tensor=t_))

    sent(wbuf.at[pl.ds(0, 28 * 128)], S_W)
    sent(xbuf.at[pl.ds(0, 3)], S_X)
    sent(xbuf.at[0, :, pl.ds(0, 512)], S_CR)
    sent(dbuf.at[:, pl.ds(0, 512)], S_DS)
    sent(hb.at[pl.ds(0, 3)], S_G)
    sent(tb.at[pl.ds(0, 3)], S_1)
    sent(abuf.at[pl.ds(0, 31)], S_REQ)
    sent(resp.at[pl.ds(0, 31)], S_RSP)

    @pl.when(inner_z)
    def _():
        sent(wbuf.at[pl.ds(0, 5 * 128)], S_Z)
        sent(dbuf.at[:, pl.ds(0, 5 * 128)], S_DZ)

    @pl.when(jnp.logical_not(inner_z))
    def _():
        sent(wbuf.at[pl.ds(0, 128)], S_Z)
        sent(dbuf.at[:, pl.ds(0, 128)], S_DZ)

    @pl.when(zh == side)
    def _():
        sent(qs.at[pl.ds(0, 3)], S_2)

    @pl.when(zh != side)
    def _():
        sent(qs, S_2)

    arrived(sb.at[pl.ds(0, 7)], R_3)
    total = sb[0]
    for t_ in range(1, 8):
        total = total + sb[t_]
    total = jnp.sum(jnp.where(turn, total, 0.0), axis=1, keepdims=True)
    norm = lax.rsqrt(total / WIDTH + 1e-05)
    for i in range(4):
        cols = slice(i * 128, i * 128 + 128)
        out_s[:, cols] = pooled[i] * norm * og_in[:, cols]
        out_s[:, i * 128 + PART : i * 128 + PART + 128] = chosen_s[:PASSES, cols]
    local(out_s, out).wait()
    sent(sb.at[pl.ds(0, 7)], S_3)


def per_device(
    states, lengths, assign, norm_gain, gate_weight, up_weight, down_weight, out_gain, centroids
):
    any_ = pl.BlockSpec(memory_space=pl.ANY)
    smem = pl.BlockSpec(memory_space=pltpu.SMEM)
    both = pl.pallas_call(
        kernel,
        out_shape=jax.ShapeDtypeStruct((PASSES, 2 * PART), F32),
        in_specs=[smem, smem] + [any_] * 7,
        out_specs=any_,
        scratch_shapes=[
            pltpu.VMEM((WIDTH, 2 * HID), BF),
            pltpu.VMEM((4, ROWS, 1024), BF),
            pltpu.VMEM((TILES, ROWS, 256), F32),
            pltpu.VMEM((OWN_ROWS, PART), BF),
            pltpu.VMEM((HID, 1024), BF),
            pltpu.VMEM((ROWS, PART), BF),
            pltpu.VMEM((128, HID), BF),
            pltpu.VMEM((128, HID), BF),
            pltpu.VMEM((32, 128), F32),
            pltpu.VMEM((1, PART), F32),
            pltpu.VMEM((ROWS, 128), F32),
            pltpu.VMEM((PAD, ROWS), BF),
            pltpu.VMEM((PAD, 128), F32),
            pltpu.VMEM((4, PAD, HID), BF),
            pltpu.VMEM((4, 4 * PASSES, 256), F32),
            pltpu.VMEM((4, 4 * PASSES, 256), BF),
            pltpu.VMEM((4, 4 * PASSES, 256), BF),
            pltpu.VMEM((4, PASSES, 256), F32),
            pltpu.VMEM((4, PASSES, 256), F32),
            pltpu.VMEM((8, 1, 128), F32),
            pltpu.VMEM((32, 1, 128), jnp.int32),
            pltpu.VMEM((256, 128), jnp.int32),
            pltpu.VMEM((256, 512), F32),
            pltpu.VMEM((32, 8, 128), F32),
            pltpu.VMEM((32, 8, 128), F32),
            pltpu.VMEM((PAD, PART), F32),
            pltpu.VMEM((PAD, PART), F32),
            pltpu.VMEM((PASSES, 2 * PART), F32),
            pltpu.SemaphoreType.DMA((S_END,)),
            pltpu.SemaphoreType.DMA((R_END,)),
            pltpu.SemaphoreType.DMA((10,)),
        ],
        compiler_params=pltpu.CompilerParams(collective_id=0, has_side_effects=True, vmem_limit_bytes=56 << 20),
        name="passages",
    )(
        lengths,
        assign,
        states.reshape(ROWS, PART),
        norm_gain.reshape(32, 128),
        gate_weight,
        up_weight,
        down_weight,
        out_gain.reshape(1, PART),
        centroids,
    )
    embedding = both[:, :PART]
    return embedding, embedding - both[:, PART:]


def solution(mesh):
    return jax.shard_map(
        per_device,
        mesh=mesh,
        in_specs=(
            P("list", None, "tensor"),
            P("list"),
            P("list"),
            P(),
            P("list", "tensor"),
            P("list", "tensor"),
            P("tensor", "list"),
            P("tensor"),
            P("list", "tensor"),
        ),
        out_specs=(P("list", "tensor"), P("list", "tensor")),
        check_vma=False,
    )
```

time: 124 us -> 109 us (0.88)
  the two profiles are of different devices: /device:TPU:6 before, /device:TPU:32 now
where the time goes in v4:
time: 109 us
  Pallas kernels  107 us (98%)
  other arithmetic  1.46 us (1%)
    pallas_call x1, Pallas kernels, per_device(): pl.pallas_call(kernel, out_shape=jax.ShapeDtypeStruct((PASSES, 2 * PART),...  107 us

profile of v4, /device:TPU:32, one launch (start us, length us, event | category | flops | bytes accessed | tf_op | source)
XLA Modules:
  0.0 109.3 jit_solution(5943888947167337535)
XLA Ops:
  0.6 107.2 %passages.1 = f32[24,1024]{1,0:T(8,128)} custom-call(s32[24]{0:T(128)} %lengths.1, s32[24]{0:T(128)} %assign.1, bf16[384,512]{1,0:T(8,128)(2,1)} %bitcast.3, f32[32,128]{1,0:T(8,128)} %bitcast.4, bf16[128,896]{1,0:T(8,128)(2,1)} %gate.1, bf16[128,896]{1,0:T(8,128)(2,1)} %up.1, bf16[896,128]{1,0:T(8,128)(2,1)} %down.1, f32[1,512]{1,0:T(1,128)} %bitcast.5, ...), custom_call_target="tpu_custom_call" | custom-call | tf_op jit(solution)/shard_map/passages/pallas_call | solution.py:477
  107.8 1.5 %slice_subtract_fusion = (f32[24,512]{1,0:T(8,128)}, f32[24,512]{1,0:T(8,128)}) fusion(f32[24,1024]{1,0:T(8,128)} %passages.1), kind=kLoop, calls=%fused_computation | loop fusion | flops 12288 | bytes 196608 | tf_op jit(solution)/shard_map/sub | solution.py:529

commit v5 on v4

--- a/solution.py
+++ b/solution.py
@@ -29,20 +29,21 @@
 R_CR = 33
 R_X = 35
 R_G = 39
-R_1 = 40
-R_2 = 41
-R_3 = 42
-R_REQ = 43
-R_RSP = 44
-R_END = 45
-S_W, S_Z, S_X, S_CR, S_DZ, S_DS, S_G, S_1, S_2, S_3, S_REQ, S_RSP, S_END = range(13)
+R_1 = 42
+R_2 = 46
+R_3 = 47
+R_REQ = 48
+R_RSP = 49
+R_MEAN = 50
+R_END = 51
+S_W, S_Z, S_X, S_CR, S_DZ, S_DS, S_G, S_1, S_2, S_3, S_REQ, S_RSP, S_MEAN, S_END = range(14)
 
 
 def kernel(
     lengths, assign, states, gain, gate, up, down, out_gain, centroids,
     out,
     wbuf, xbuf, acc, cbuf, dbuf, sbuf, g_in, u_in, gain_in, og_in,
-    scale_s, mask_s, inv_s, hb, tf, tb, r1b, qs, rb, sb, abuf, pick, cacc, resp, gotc, chosen_s, smean, out_s,
+    scale_s, mask_s, inv_s, hb, tf, tb, r1b, qs, rb, rb7, mine_m, other_m, sb, abuf, pick, cacc, resp, gotc, chosen_s, smean, out_s,
     ss, rs, ls,
 ):
     lst = lax.axis_index("list")
@@ -116,16 +117,16 @@
     def greet_list(i):
         pl.semaphore_signal(barrier, inc=1, device_id=dev(list_=lax.rem(lst + i, 32)), device_id_type=MESH)
 
-    def greet_tensor(i):
-        pl.semaphore_signal(barrier, inc=1, device_id=dev(tensor=lax.rem(ten + i, 8)), device_id_type=MESH)
+    def greet_x(i):
+        pl.semaphore_signal(barrier, inc=1, device_id=dev(tensor=lax.rem(ten + 2 * i, 8)), device_id_type=MESH)
 
     def greet_across(i):
         there = dev(list_=zl * 8 + lax.rem(y + i, 4) * 2 + core, tensor=x * 2 + 1 - zh)
         pl.semaphore_signal(barrier, inc=1, device_id=there, device_id_type=MESH)
 
+    pl.loop(0, 4)(greet_across)
+    pl.loop(1, 4)(greet_x)
     pl.loop(1, 32)(greet_list)
-    pl.loop(1, 8)(greet_tensor)
-    pl.loop(1, 4)(greet_across)
     for cp in cps_w:
         cp.wait()
     eye = lax.broadcasted_iota(jnp.int32, (128, 128), 0) == lax.broadcasted_iota(jnp.int32, (128, 128), 1)
@@ -135,7 +136,7 @@
         wbuf[own_rows, j * 256 : j * 256 + 128] = (g_in[:, j * 128 : j * 128 + 128].astype(F32) * gcol).astype(BF)
         wbuf[own_rows, j * 256 + 128 : j * 256 + 256] = (u_in[:, j * 128 : j * 128 + 128].astype(F32) * gcol).astype(BF)
 
-    pl.semaphore_wait(barrier, 31 + 7 + 3)
+    pl.semaphore_wait(barrier, 31 + 3 + 4)
     for step in (1, -1, 2):
         for half in range(2):
             send(states.at[:, pl.ds(half * 256, 256)], xslot(zh, half, x), S_X, R_X + half, at_x(step))
@@ -233,6 +234,9 @@
     def from_sibling_halves(k):
         arrived(wblock(y_of(2), place(k), 1 - core), R_SH + k)
 
+    def packed(v):
+        return jnp.concatenate([v[:, :128], v[:, 128:]], axis=0)
+
     column(0)
 
     lane = lax.broadcasted_iota(jnp.int32, (1, 128), 1)
@@ -259,9 +263,11 @@
     inv_s[...] = 1.0 / lcol.astype(F32)
     cp_s.wait()
     smean[...] = jnp.dot(mask_s[...], sbuf[...], preferred_element_type=F32) * inv_s[:, :1]
+    for i in range(2):
+        mine_m[i] = packed(smean[:PASSES, i * 256 : i * 256 + 256]).astype(BF)
+    send(mine_m, other_m, S_MEAN, R_MEAN, partner)
 
     column(1)
-    cross(0)
     pl.when(inner_z)(lambda: column(2))
     neighbour(0)
 
@@ -297,11 +303,11 @@
         peer = lax.rem(lst + i, 32)
         send(resp.at[peer], gotc.at[lst], S_RSP, R_RSP, dev(list_=peer))
 
+    cross(0)
     outer_z = jnp.logical_not(inner_z)
     pl.when(inner_z)(lambda: column(3))
     neighbour(1)
     pl.when(outer_z)(lambda: column(2))
-    cross(1)
     for cp in cps_x:
         cp.wait()
     for half in range(2):
@@ -316,8 +322,10 @@
     for k in range(2):
         from_sibling_neighbours(k)
         product(y_a, k)
+    pl.when(inner_z)(lambda: cross(1))
     neighbour(2)
-    pl.when(jnp.logical_not(inner_z))(lambda: column(3))
+    pl.when(outer_z)(lambda: column(3))
+    pl.when(outer_z)(lambda: cross(1))
     crossed(1)
     down_column(0)
     halves(1)
@@ -328,15 +336,18 @@
         from_sibling_column(k)
         product(y, k)
     squares_of((1 - zh) * 2 + lax.rem(y, 2), False)
-    neighbour(3)
     halves(2)
+    for k in range(2):
+        from_sibling_halves(k)
+        product(y_of(2), k)
     down_column(1)
     pl.when(inner_z)(lambda: down_column(2))
-    for k in range(3):
-        from_sibling_halves(k)
-        product(y_of(2), k)
+    neighbour(3)
+    from_sibling_halves(2)
+    product(y_of(2), 2)
     from_sibling_neighbours(3)
     product(y_a, 3)
+    pl.when(inner_z)(lambda: down_column(3))
     x_arrived(3)
     squares_of((1 - zh) * 2 + lax.rem(y + 1, 2), False)
     for k in range(4):
@@ -345,8 +356,14 @@
         lax.rsqrt(jnp.sum(scale_s[...], axis=1, keepdims=True) / WIDTH + 1e-05), (ROWS, 128)
     )
     halves(3)
-    pl.when(inner_z)(lambda: down_column(3))
     from_sibling_halves(3)
+    around = (2, 1, -1)
+
+    def send_pooled(start, width):
+        for n, step in enumerate(around):
+            part = hb.at[y, :, pl.ds(start, width)]
+            send(part, part, S_G, R_G + n, at_y(step))
+
     yy = y_of(2)
     ks = pl.ds(pl.multiple_of(place(3) * 256, 256), 256)
     wrows = pl.ds(pl.multiple_of(yy * 1024 + place(3) * 256, 256), 256)
@@ -354,16 +371,18 @@
         r = acc[j] + jnp.dot(xbuf[yy, :, ks], wbuf[wrows, j * 256 : j * 256 + 256], preferred_element_type=F32)
         g = r[:, :128] * scale_s[...]
         u = r[:, 128:] * scale_s[...]
-        h = (g / (1.0 + jnp.exp(-g)) * u).astype(BF)
+        h = (g * (0.5 + 0.5 * jnp.tanh(0.5 * g)) * u).astype(BF)
         pooled_h = jnp.dot(mask_s[...], h, preferred_element_type=F32) * inv_s[...]
         hb[y, :, j * 128 : j * 128 + 128] = pooled_h.astype(BF)
-
-    for step in (1, -1, 2):
-        send(hb.at[y], hb.at[y], S_G, R_G, at_y(step))
-    @pl.when(jnp.logical_not(inner_z))
+        if j == 3:
+            send_pooled(0, 512)
+
+    send_pooled(512, HID - 512)
+    @pl.when(outer_z)
     def _():
         down_column(2)
         down_column(3)
+
 
     arrived(dbuf.at[:, pl.ds(0, 512)], R_DS)
     cp_o.wait()
@@ -379,55 +398,47 @@
         one = jnp.where(wide == own_col[:, :1] * 8 + q * 2 + slot, 1.0, 0.0).astype(BF)
         chosen_s[:, q * 128 : q * 128 + 128] = jnp.dot(one, table, preferred_element_type=F32)
 
-    arrived(hb.at[pl.ds(0, 3)], R_G)
-
-    for z_ in range(4):
-        term = jnp.dot(hb[...].reshape(4 * PAD, HID), dbuf[:, z_ * 256 : z_ * 256 + 256], preferred_element_type=F32)
-        term = jnp.concatenate([term[g * PAD : g * PAD + PASSES] for g in range(4)], axis=0)
-        tf[z_] = term
-        tb[z_] = term.astype(BF)
-    for step in (1, -1, 2):
-        x_ = lax.rem(x + step + 4, 4)
-        send(tb.at[x_], r1b.at[x], S_1, R_1, at_x(step))
-    arrived(r1b.at[pl.ds(0, 3)], R_1)
-    q_sum = tf[x]
-    for step in (1, -1, 2):
-        x_ = lax.rem(x + step + 4, 4)
-        q_sum = q_sum + r1b[x_].astype(F32)
-    qs[...] = q_sum.reshape(4, PASSES, 256)
-    slot2 = zh * 2 + lax.rem(y, 2)
-    side = y // 2
-    for step in (0, 1, -1, 2):
+
+    passes_y = ((0, 0), (1, 2), (-1, 1), (2, 0))
+    for n, (step, came) in enumerate(passes_y):
         y_ = y_of(step)
-        target = dev(list_=zl * 8 + y_ * 2 + core, tensor=x * 2 + side)
-        cond = (zh != side) if step == 0 else None
-        send(qs.at[y_], rb.at[slot2], S_2, R_2, target, cond)
-
-    @pl.when(zh == side)
-    def _():
-        rb[slot2] = qs[y]
-
-    @pl.when(zh == side)
-    def _():
-        arrived(rb.at[pl.ds(0, 3)], R_2)
-
-    @pl.when(zh != side)
-    def _():
-        arrived(rb, R_2)
-
+        if step != 0:
+            arrived(hb.at[y_], R_G + came)
+        term = jnp.dot(hb[y_], dbuf[...], preferred_element_type=F32)
+        for z_ in range(4):
+            v = packed(term[:PASSES, z_ * 256 : z_ * 256 + 256])
+            tf[z_, y_] = v
+            tb[z_, y_] = v.astype(BF)
+        for x_step in (2, 1, -1):
+            x_ = lax.rem(x + x_step + 4, 4)
+            send(tb.at[x_, y_], r1b.at[x, y_], S_1, R_1 + n, at_x(x_step))
+    for n, (step, _) in enumerate(passes_y):
+        y_ = y_of(step)
+        arrived(r1b.at[pl.ds(0, 3), 0], R_1 + n)
+        v = tf[x, y_]
+        for x_step in (1, -1, 2):
+            v = v + r1b[lax.rem(x + x_step + 4, 4), y_].astype(F32)
+        qs[y_] = v.astype(BF)
+        for far in (1, 0):
+            if step == 0 and far == 0:
+                rb[zh, y] = qs[y]
+            else:
+                target = dev(list_=zl * 8 + y_ * 2 + core, tensor=x * 2 + lax.rem(zh + far, 2))
+                send(qs.at[y_], rb.at[zh, y], S_2, R_2, target)
+    arrived(other_m, R_MEAN)
+    arrived(rb7.at[pl.ds(0, 7)], R_2)
     pooled = []
     squares = jnp.zeros((PASSES, 128), F32)
-    for i in range(4):
-        half = slice(i % 2 * 128, i % 2 * 128 + 128)
-        v = smean[:PASSES, i * 128 : i * 128 + 128] + rb[i // 2, :, half] + rb[2 + i // 2, :, half]
-        squares = squares + v * v
-        pooled.append(v)
+    for i in range(2):
+        v = rb[0, zh * 2 + i].astype(F32) + rb[1, zh * 2 + i].astype(F32) + packed(smean[:PASSES, i * 256 : i * 256 + 256])
+        w = rb[0, (1 - zh) * 2 + i].astype(F32) + rb[1, (1 - zh) * 2 + i].astype(F32) + other_m[i].astype(F32)
+        both = v * v + w * w
+        squares = squares + both[:PASSES] + both[PASSES:]
+        pooled += [v[:PASSES], v[PASSES:]]
     turn = lax.broadcasted_iota(jnp.int32, (PASSES, 128), 0) == lax.broadcasted_iota(jnp.int32, (PASSES, 128), 1)
-    sb[ten] = jnp.sum(jnp.where(turn, jnp.sum(squares, axis=1, keepdims=True), 0.0), axis=0, keepdims=True)
-    for i in range(1, 8):
-        t_ = lax.rem(ten + i, 8)
-        send(sb.at[ten], sb.at[ten], S_3, R_3, dev(tensor=t_))
-
+    sb[x] = jnp.sum(jnp.where(turn, jnp.sum(squares, axis=1, keepdims=True), 0.0), axis=0, keepdims=True)
+    for step in (2, 1, -1):
+        send(sb.at[x], sb.at[x], S_3, R_3, at_x(step))
     sent(wbuf.at[pl.ds(0, 28 * 128)], S_W)
     sent(xbuf.at[pl.ds(0, 3)], S_X)
     sent(xbuf.at[0, :, pl.ds(0, 512)], S_CR)
@@ -447,18 +458,12 @@
         sent(wbuf.at[pl.ds(0, 128)], S_Z)
         sent(dbuf.at[:, pl.ds(0, 128)], S_DZ)
 
-    @pl.when(zh == side)
-    def _():
-        sent(qs.at[pl.ds(0, 3)], S_2)
-
-    @pl.when(zh != side)
-    def _():
-        sent(qs, S_2)
-
-    arrived(sb.at[pl.ds(0, 7)], R_3)
+    sent(rb7.at[pl.ds(0, 7)], S_2)
+    sent(mine_m, S_MEAN)
+    arrived(sb.at[pl.ds(0, 3)], R_3)
     total = sb[0]
-    for t_ in range(1, 8):
-        total = total + sb[t_]
+    for x_ in range(1, 4):
+        total = total + sb[x_]
     total = jnp.sum(jnp.where(turn, total, 0.0), axis=1, keepdims=True)
     norm = lax.rsqrt(total / WIDTH + 1e-05)
     for i in range(4):
@@ -466,7 +471,7 @@
         out_s[:, cols] = pooled[i] * norm * og_in[:, cols]
         out_s[:, i * 128 + PART : i * 128 + PART + 128] = chosen_s[:PASSES, cols]
     local(out_s, out).wait()
-    sent(sb.at[pl.ds(0, 7)], S_3)
+    sent(sb.at[pl.ds(0, 3)], S_3)
 
 
 def per_device(
@@ -494,12 +499,15 @@
             pltpu.VMEM((PAD, ROWS), BF),
             pltpu.VMEM((PAD, 128), F32),
             pltpu.VMEM((4, PAD, HID), BF),
-            pltpu.VMEM((4, 4 * PASSES, 256), F32),
-            pltpu.VMEM((4, 4 * PASSES, 256), BF),
-            pltpu.VMEM((4, 4 * PASSES, 256), BF),
-            pltpu.VMEM((4, PASSES, 256), F32),
-            pltpu.VMEM((4, PASSES, 256), F32),
-            pltpu.VMEM((8, 1, 128), F32),
+            pltpu.VMEM((4, 4, 2 * PASSES, 128), F32),
+            pltpu.VMEM((4, 4, 2 * PASSES, 128), BF),
+            pltpu.VMEM((4, 4, 2 * PASSES, 128), BF),
+            pltpu.VMEM((4, 2 * PASSES, 128), BF),
+            pltpu.VMEM((2, 4, 2 * PASSES, 128), BF),
+            pltpu.VMEM((8, 2 * PASSES, 128), BF),
+            pltpu.VMEM((2, 2 * PASSES, 128), BF),
+            pltpu.VMEM((2, 2 * PASSES, 128), BF),
+            pltpu.VMEM((4, 1, 128), F32),
             pltpu.VMEM((32, 1, 128), jnp.int32),
             pltpu.VMEM((256, 128), jnp.int32),
             pltpu.VMEM((256, 512), F32),

time: 109 us -> 101 us (0.927)
  the two profiles are of different devices: /device:TPU:32 before, /device:TPU:6 now
where the time goes in v5:
time: 101 us; the launch traced here: 99.7 us
  Pallas kernels  97.6 us (97%)
  other arithmetic  1.46 us (1%)
    pallas_call x1, Pallas kernels, per_device(): pl.pallas_call(kernel, out_shape=jax.ShapeDtypeStruct((PASSES, 2 * PART),...  97.6 us

profile of v5, /device:TPU:6, one launch (start us, length us, event | category | flops | bytes accessed | tf_op | source)
XLA Modules:
  0.0 99.7 jit_solution(10290478862346067383)
XLA Ops:
  0.6 97.6 %passages.1 = f32[24,1024]{1,0:T(8,128)} custom-call(s32[24]{0:T(128)} %lengths.1, s32[24]{0:T(128)} %assign.1, bf16[384,512]{1,0:T(8,128)(2,1)} %bitcast.3, f32[32,128]{1,0:T(8,128)} %bitcast.4, bf16[128,896]{1,0:T(8,128)(2,1)} %gate.1, bf16[128,896]{1,0:T(8,128)(2,1)} %up.1, bf16[896,128]{1,0:T(8,128)(2,1)} %down.1, f32[1,512]{1,0:T(1,128)} %bitcast.5, ...), custom_call_target="tpu_custom_call" | custom-call | tf_op jit(solution)/shard_map/passages/pallas_call | solution.py:482
  98.3 1.5 %slice_subtract_fusion = (f32[24,512]{1,0:T(8,128)}, f32[24,512]{1,0:T(8,128)}) fusion(f32[24,1024]{1,0:T(8,128)} %passages.1), kind=kLoop, calls=%fused_computation | loop fusion | flops 12288 | bytes 196608 | tf_op jit(solution)/shard_map/sub | solution.py:537

commit v6 on v5

--- a/solution.py
+++ b/solution.py
@@ -35,15 +35,18 @@
 R_REQ = 48
 R_RSP = 49
 R_MEAN = 50
-R_END = 51
-S_W, S_Z, S_X, S_CR, S_DZ, S_DS, S_G, S_1, S_2, S_3, S_REQ, S_RSP, S_MEAN, S_END = range(14)
+R_CB = 51
+R_XB = 53
+R_G2 = 55
+R_END = 58
+S_W, S_Z, S_X, S_CR, S_DZ, S_DS, S_G, S_1, S_2, S_3, S_REQ, S_RSP, S_MEAN, S_G2, S_END = range(15)
 
 
 def kernel(
     lengths, assign, states, gain, gate, up, down, out_gain, centroids,
     out,
     wbuf, xbuf, acc, cbuf, dbuf, sbuf, g_in, u_in, gain_in, og_in,
-    scale_s, mask_s, inv_s, hb, tf, tb, r1b, qs, rb, rb7, mine_m, other_m, sb, abuf, pick, cacc, resp, gotc, chosen_s, smean, out_s,
+    scale_s, mask_s, inv_s, hb, hb2, hid, tf, tb, r1b, qs, rb, rb7, mine_m, other_m, sb, abuf, pick, cacc, resp, gotc, chosen_s, smean, out_s,
     ss, rs, ls,
 ):
     lst = lax.axis_index("list")
@@ -141,16 +144,20 @@
         for half in range(2):
             send(states.at[:, pl.ds(half * 256, 256)], xslot(zh, half, x), S_X, R_X + half, at_x(step))
 
-    def cross(n):
-        half = lax.rem(y + n, 2)
-        send(states.at[:, pl.ds(pl.multiple_of(half * 256, 256), 256)], xslot(zh, half, x), S_CR, R_CR + n, partner)
-
-    def crossed(n):
-        half = lax.rem(y + n, 2)
-        block = xslot(1 - zh, half, x)
-        arrived(block, R_CR + n)
+    def piece(z_hi, n, p, x_):
+        rows = pl.ds(0, ROWS) if n == 0 else pl.ds(p * (ROWS // 2), ROWS // 2)
+        return xbuf.at[z_hi * 2 + lax.rem(y + n, 2), rows, pl.ds(pl.multiple_of(x_ * 256, 256), 256)]
+
+    def cross(n, p=0):
+        rows = pl.ds(0, ROWS) if n == 0 else pl.ds(p * (ROWS // 2), ROWS // 2)
+        cols = pl.ds(pl.multiple_of(lax.rem(y + n, 2) * 256, 256), 256)
+        send(states.at[rows, cols], piece(zh, n, p, x), S_CR, R_CR if n == 0 else R_CB + p, partner)
+
+    def crossed(n, p=0):
+        block = piece(1 - zh, n, p, x)
+        arrived(block, R_CR if n == 0 else R_CB + p)
         for step in (1, -1, 2):
-            send(block, block, S_X, R_X + 2 + n, at_x(step))
+            send(block, block, S_X, R_X + 2 if n == 0 else R_XB + p, at_x(step))
 
     def x_arrived(n):
         arrived(xbuf.at[0, :, pl.ds(0, 768)], R_X + n)
@@ -196,18 +203,21 @@
         arrived(block, R_H + k)
         send(block, block, S_W, R_SH + k, sibling)
 
-    def down_column(k):
-        z_ = place(k)
+    outer_z = jnp.logical_not(inner_z)
+    near_end = jnp.where(zl < 2, 0, 3)
+    near_mid = jnp.where(zl < 2, 1, 2)
+
+    def down_to(z_, to):
         block = dslot(z_, core)
-        if k == 0:
-            cp_d.wait()
-            send(block, block, S_DZ, R_DN + z_, at_z(lax.rem(zl + 1, 4)), zl < 3)
-            send(block, block, S_DZ, R_DN + z_, at_z(lax.rem(zl + 3, 4)), zl > 0)
-        else:
-            arrived(block, R_DN + z_)
-            onward = jnp.where(z_ < zl, zl + 1, zl - 1)
-            send(block, block, S_DZ, R_DN + z_, at_z(lax.rem(onward + 4, 4)), inner_z)
+        send(block, block, S_DZ, R_DN + z_, at_z(to))
+
+    def down_over(z_):
+        block = dslot(z_, core)
         send(block, block, S_DS, R_DS, sibling)
+
+    def down_from(z_):
+        arrived(dslot(z_, core), R_DN + z_)
+        down_over(z_)
 
     def product(yy, k):
         ks = pl.ds(pl.multiple_of(place(k) * 256, 256), 256)
@@ -304,7 +314,6 @@
         send(resp.at[peer], gotc.at[lst], S_RSP, R_RSP, dev(list_=peer))
 
     cross(0)
-    outer_z = jnp.logical_not(inner_z)
     pl.when(inner_z)(lambda: column(3))
     neighbour(1)
     pl.when(outer_z)(lambda: column(2))
@@ -322,12 +331,20 @@
     for k in range(2):
         from_sibling_neighbours(k)
         product(y_a, k)
-    pl.when(inner_z)(lambda: cross(1))
+    cp_d.wait()
+    down_to(zl, jnp.where(inner_z, 3 - zl, near_mid))
+    down_over(zl)
+    cross(1, 0)
     neighbour(2)
     pl.when(outer_z)(lambda: column(3))
-    pl.when(outer_z)(lambda: cross(1))
-    crossed(1)
-    down_column(0)
+    cross(1, 1)
+    @pl.when(inner_z)
+    def _():
+        down_from(near_end)
+        down_to(near_end, 3 - zl)
+        down_to(zl, near_end)
+
+    crossed(1, 0)
     halves(1)
     from_sibling_neighbours(2)
     product(y_a, 2)
@@ -335,54 +352,62 @@
     for k in range(4):
         from_sibling_column(k)
         product(y, k)
+    crossed(1, 1)
+    @pl.when(inner_z)
+    def _():
+        down_from(3 - zl)
+        down_to(3 - zl, near_end)
+
     squares_of((1 - zh) * 2 + lax.rem(y, 2), False)
     halves(2)
     for k in range(2):
         from_sibling_halves(k)
         product(y_of(2), k)
-    down_column(1)
-    pl.when(inner_z)(lambda: down_column(2))
     neighbour(3)
+    @pl.when(inner_z)
+    def _():
+        down_from(3 - near_end)
+        down_to(3 - near_end, near_end)
+
     from_sibling_halves(2)
     product(y_of(2), 2)
     from_sibling_neighbours(3)
     product(y_a, 3)
-    pl.when(inner_z)(lambda: down_column(3))
-    x_arrived(3)
+    for p in range(2):
+        arrived(xbuf.at[0, pl.ds(0, ROWS // 2), pl.ds(0, 768)], R_XB + p)
     squares_of((1 - zh) * 2 + lax.rem(y + 1, 2), False)
-    for k in range(4):
-        product(y_b, k)
+    product(y_b, 0)
+    product(y_b, 1)
+    halves(3)
+    product(y_b, 2)
+    product(y_b, 3)
     scale_s[...] = jnp.broadcast_to(
         lax.rsqrt(jnp.sum(scale_s[...], axis=1, keepdims=True) / WIDTH + 1e-05), (ROWS, 128)
     )
-    halves(3)
     from_sibling_halves(3)
     around = (2, 1, -1)
-
-    def send_pooled(start, width):
-        for n, step in enumerate(around):
-            part = hb.at[y, :, pl.ds(start, width)]
-            send(part, part, S_G, R_G + n, at_y(step))
 
     yy = y_of(2)
     ks = pl.ds(pl.multiple_of(place(3) * 256, 256), 256)
     wrows = pl.ds(pl.multiple_of(yy * 1024 + place(3) * 256, 256), 256)
-    for j in range(TILES):
-        r = acc[j] + jnp.dot(xbuf[yy, :, ks], wbuf[wrows, j * 256 : j * 256 + 256], preferred_element_type=F32)
-        g = r[:, :128] * scale_s[...]
-        u = r[:, 128:] * scale_s[...]
-        h = (g * (0.5 + 0.5 * jnp.tanh(0.5 * g)) * u).astype(BF)
-        pooled_h = jnp.dot(mask_s[...], h, preferred_element_type=F32) * inv_s[...]
-        hb[y, :, j * 128 : j * 128 + 128] = pooled_h.astype(BF)
-        if j == 3:
-            send_pooled(0, 512)
-
-    send_pooled(512, HID - 512)
+    for first, last_, buf, kind, recv in ((0, 4, hb, S_G, R_G), (4, TILES, hb2, S_G2, R_G2)):
+        for j in range(first, last_):
+            r = acc[j] + jnp.dot(xbuf[yy, :, ks], wbuf[wrows, j * 256 : j * 256 + 256], preferred_element_type=F32)
+            g = r[:, :128] * scale_s[...]
+            u = r[:, 128:] * scale_s[...]
+            hid[:, j * 128 : j * 128 + 128] = (g * (0.5 + 0.5 * jnp.tanh(0.5 * g)) * u).astype(BF)
+        p = jnp.dot(mask_s[...], hid[:, first * 128 : last_ * 128], preferred_element_type=F32)
+        rows_p = [p[:PASSES, i * 128 : i * 128 + 128] * inv_s[:PASSES] for i in range(last_ - first)]
+        if first:
+            rows_p.append(jnp.zeros((8, 128), F32))
+        buf[y] = jnp.concatenate(rows_p, axis=0).astype(BF)
+        for n, step in enumerate(around):
+            send(buf.at[y], buf.at[y], kind, recv + n, at_y(step))
     @pl.when(outer_z)
     def _():
-        down_column(2)
-        down_column(3)
-
+        down_from(near_mid)
+        down_from(3 - near_mid)
+        down_from(3 - zl)
 
     arrived(dbuf.at[:, pl.ds(0, 512)], R_DS)
     cp_o.wait()
@@ -404,9 +429,13 @@
         y_ = y_of(step)
         if step != 0:
             arrived(hb.at[y_], R_G + came)
-        term = jnp.dot(hb[y_], dbuf[...], preferred_element_type=F32)
+            arrived(hb2.at[y_], R_G2 + came)
+        a, b = hb[y_].astype(F32), hb2[y_].astype(F32)
+        parts = [a[i * PASSES : i * PASSES + PASSES] for i in range(4)] + [b[i * PASSES : i * PASSES + PASSES] for i in range(3)]
+        rows_in = jnp.concatenate(parts, axis=1).astype(BF)
+        term = jnp.dot(rows_in, dbuf[...], preferred_element_type=F32)
         for z_ in range(4):
-            v = packed(term[:PASSES, z_ * 256 : z_ * 256 + 256])
+            v = packed(term[:, z_ * 256 : z_ * 256 + 256])
             tf[z_, y_] = v
             tb[z_, y_] = v.astype(BF)
         for x_step in (2, 1, -1):
@@ -444,6 +473,7 @@
     sent(xbuf.at[0, :, pl.ds(0, 512)], S_CR)
     sent(dbuf.at[:, pl.ds(0, 512)], S_DS)
     sent(hb.at[pl.ds(0, 3)], S_G)
+    sent(hb2.at[pl.ds(0, 3)], S_G2)
     sent(tb.at[pl.ds(0, 3)], S_1)
     sent(abuf.at[pl.ds(0, 31)], S_REQ)
     sent(resp.at[pl.ds(0, 31)], S_RSP)
@@ -468,9 +498,8 @@
     norm = lax.rsqrt(total / WIDTH + 1e-05)
     for i in range(4):
         cols = slice(i * 128, i * 128 + 128)
-        out_s[:, cols] = pooled[i] * norm * og_in[:, cols]
-        out_s[:, i * 128 + PART : i * 128 + PART + 128] = chosen_s[:PASSES, cols]
-    local(out_s, out).wait()
+        out[:, cols] = pooled[i] * norm * og_in[:, cols]
+        out[:, i * 128 + PART : i * 128 + PART + 128] = chosen_s[:PASSES, cols]
     sent(sb.at[pl.ds(0, 3)], S_3)
 
 
@@ -481,9 +510,9 @@
     smem = pl.BlockSpec(memory_space=pltpu.SMEM)
     both = pl.pallas_call(
         kernel,
-        out_shape=jax.ShapeDtypeStruct((PASSES, 2 * PART), F32),
+        out_shape=pltpu.VMEM((PASSES, 2 * PART), F32),
         in_specs=[smem, smem] + [any_] * 7,
-        out_specs=any_,
+        out_specs=pl.BlockSpec(memory_space=pltpu.VMEM),
         scratch_shapes=[
             pltpu.VMEM((WIDTH, 2 * HID), BF),
             pltpu.VMEM((4, ROWS, 1024), BF),
@@ -498,7 +527,9 @@
             pltpu.VMEM((ROWS, 128), F32),
             pltpu.VMEM((PAD, ROWS), BF),
             pltpu.VMEM((PAD, 128), F32),
-            pltpu.VMEM((4, PAD, HID), BF),
+            pltpu.VMEM((4, 4 * PASSES, 128), BF),
+            pltpu.VMEM((4, 3 * PASSES + 8, 128), BF),
+            pltpu.VMEM((ROWS, HID), BF),
             pltpu.VMEM((4, 4, 2 * PASSES, 128), F32),
             pltpu.VMEM((4, 4, 2 * PASSES, 128), BF),
             pltpu.VMEM((4, 4, 2 * PASSES, 128), BF),

time: 101 us -> 98.9 us (0.979)
  Pallas kernels: 97.6 us -> 96.3 us
    pallas_call x1, Pallas kernels: 97.6 us -> 96.3 us  [per_device(): pl.pallas_call(kernel, out_shape=pltpu.VMEM((PASSES, 2 * PART), F32), in_...]
where the time goes in v6:
time: 98.9 us; the launch traced here: 97.6 us
  Pallas kernels  96.3 us (97%)
    pallas_call x1, Pallas kernels, per_device(): pl.pallas_call(kernel, out_shape=pltpu.VMEM((PASSES, 2 * PART), F32), in_...  96.3 us

profile of v6, /device:TPU:6, one launch (start us, length us, event | category | flops | bytes accessed | tf_op | source)
XLA Modules:
  0.0 97.6 jit_solution(14997828441029295906)
XLA Ops:
  0.6 96.3 %passages.1 = f32[24,1024]{1,0:T(8,128)S(1)} custom-call(s32[24]{0:T(128)} %lengths.1, s32[24]{0:T(128)} %assign.1, bf16[384,512]{1,0:T(8,128)(2,1)} %bitcast.3, f32[32,128]{1,0:T(8,128)} %bitcast.4, bf16[128,896]{1,0:T(8,128)(2,1)} %gate.1, bf16[128,896]{1,0:T(8,128)(2,1)} %up.1, bf16[896,128]{1,0:T(8,128)(2,1)} %down.1, f32[1,512]{1,0:T(1,128)} %bitcast.5, ...), custom_call_target="tpu_custom_call" | custom-call | tf_op jit(solution)/shard_map/passages/pallas_call | solution.py:511
  96.9 0.6 slice_subtract_fusion

commit v7 on v6

--- a/solution.py
+++ b/solution.py
@@ -127,7 +127,7 @@
         there = dev(list_=zl * 8 + lax.rem(y + i, 4) * 2 + core, tensor=x * 2 + 1 - zh)
         pl.semaphore_signal(barrier, inc=1, device_id=there, device_id_type=MESH)
 
-    pl.loop(0, 4)(greet_across)
+    greet_across(0)
     pl.loop(1, 4)(greet_x)
     pl.loop(1, 32)(greet_list)
     for cp in cps_w:
@@ -139,7 +139,7 @@
         wbuf[own_rows, j * 256 : j * 256 + 128] = (g_in[:, j * 128 : j * 128 + 128].astype(F32) * gcol).astype(BF)
         wbuf[own_rows, j * 256 + 128 : j * 256 + 256] = (u_in[:, j * 128 : j * 128 + 128].astype(F32) * gcol).astype(BF)
 
-    pl.semaphore_wait(barrier, 31 + 3 + 4)
+    pl.semaphore_wait(barrier, 31 + 3 + 1)
     for step in (1, -1, 2):
         for half in range(2):
             send(states.at[:, pl.ds(half * 256, 256)], xslot(zh, half, x), S_X, R_X + half, at_x(step))
@@ -281,6 +281,7 @@
     pl.when(inner_z)(lambda: column(2))
     neighbour(0)
 
+    pl.when(jnp.logical_not(inner_z))(lambda: cross(0))
     arrived(abuf.at[pl.ds(0, 31)], R_REQ)
     cp_c.wait()
     wanted = jnp.broadcast_to(abuf[...], (32, 8, 128))
@@ -313,7 +314,7 @@
         peer = lax.rem(lst + i, 32)
         send(resp.at[peer], gotc.at[lst], S_RSP, R_RSP, dev(list_=peer))
 
-    cross(0)
+    pl.when(inner_z)(lambda: cross(0))
     pl.when(inner_z)(lambda: column(3))
     neighbour(1)
     pl.when(outer_z)(lambda: column(2))
@@ -378,9 +379,9 @@
     squares_of((1 - zh) * 2 + lax.rem(y + 1, 2), False)
     product(y_b, 0)
     product(y_b, 1)
-    halves(3)
     product(y_b, 2)
     product(y_b, 3)
+    halves(3)
     scale_s[...] = jnp.broadcast_to(
         lax.rsqrt(jnp.sum(scale_s[...], axis=1, keepdims=True) / WIDTH + 1e-05), (ROWS, 128)
     )
@@ -424,36 +425,44 @@
         chosen_s[:, q * 128 : q * 128 + 128] = jnp.dot(one, table, preferred_element_type=F32)
 
 
-    passes_y = ((0, 0), (1, 2), (-1, 1), (2, 0))
-    for n, (step, came) in enumerate(passes_y):
-        y_ = y_of(step)
-        if step != 0:
-            arrived(hb.at[y_], R_G + came)
-            arrived(hb2.at[y_], R_G2 + came)
-        a, b = hb[y_].astype(F32), hb2[y_].astype(F32)
-        parts = [a[i * PASSES : i * PASSES + PASSES] for i in range(4)] + [b[i * PASSES : i * PASSES + PASSES] for i in range(3)]
-        rows_in = jnp.concatenate(parts, axis=1).astype(BF)
+    steps = (0, 1, -1, 2)
+    came = {1: 2, -1: 1, 2: 0}
+    groups = ((0, 1), (1, 3), (3, 4))
+    for n, (lo, hi) in enumerate(groups):
+        rows_in = []
+        for step in steps[lo:hi]:
+            y_ = y_of(step)
+            if step != 0:
+                arrived(hb.at[y_], R_G + came[step])
+                arrived(hb2.at[y_], R_G2 + came[step])
+            a, b = hb[y_].astype(F32), hb2[y_].astype(F32)
+            parts = [a[i * PASSES : i * PASSES + PASSES] for i in range(4)] + [b[i * PASSES : i * PASSES + PASSES] for i in range(3)]
+            rows_in.append(jnp.concatenate(parts, axis=1))
+        rows_in = (rows_in[0] if len(rows_in) == 1 else jnp.concatenate(rows_in, axis=0)).astype(BF)
         term = jnp.dot(rows_in, dbuf[...], preferred_element_type=F32)
-        for z_ in range(4):
-            v = packed(term[:, z_ * 256 : z_ * 256 + 256])
-            tf[z_, y_] = v
-            tb[z_, y_] = v.astype(BF)
+        for m in range(lo, hi):
+            for z_ in range(4):
+                v = packed(term[(m - lo) * PASSES : (m - lo + 1) * PASSES, z_ * 256 : z_ * 256 + 256])
+                tf[z_, m] = v
+                tb[z_, m] = v.astype(BF)
         for x_step in (2, 1, -1):
             x_ = lax.rem(x + x_step + 4, 4)
-            send(tb.at[x_, y_], r1b.at[x, y_], S_1, R_1 + n, at_x(x_step))
-    for n, (step, _) in enumerate(passes_y):
-        y_ = y_of(step)
-        arrived(r1b.at[pl.ds(0, 3), 0], R_1 + n)
-        v = tf[x, y_]
-        for x_step in (1, -1, 2):
-            v = v + r1b[lax.rem(x + x_step + 4, 4), y_].astype(F32)
-        qs[y_] = v.astype(BF)
-        for far in (1, 0):
-            if step == 0 and far == 0:
-                rb[zh, y] = qs[y]
-            else:
-                target = dev(list_=zl * 8 + y_ * 2 + core, tensor=x * 2 + lax.rem(zh + far, 2))
-                send(qs.at[y_], rb.at[zh, y], S_2, R_2, target)
+            here = pl.ds(lo, hi - lo)
+            send(tb.at[x_, here], r1b.at[x, here], S_1, R_1 + n, at_x(x_step))
+    for n, (lo, hi) in enumerate(groups):
+        arrived(r1b.at[pl.ds(0, 3), pl.ds(0, hi - lo)], R_1 + n)
+        for m in range(lo, hi):
+            y_ = y_of(steps[m])
+            v = tf[x, m]
+            for x_step in (1, -1, 2):
+                v = v + r1b[lax.rem(x + x_step + 4, 4), m].astype(F32)
+            qs[y_] = v.astype(BF)
+            for far in (1, 0):
+                if m == 0 and far == 0:
+                    rb[zh, y] = qs[y]
+                else:
+                    target = dev(list_=zl * 8 + y_ * 2 + core, tensor=x * 2 + lax.rem(zh + far, 2))
+                    send(qs.at[y_], rb.at[zh, y], S_2, R_2, target)
     arrived(other_m, R_MEAN)
     arrived(rb7.at[pl.ds(0, 7)], R_2)
     pooled = []

time: 98.9 us -> 98.7 us (level)
  no operation moved by 1% of the time
where the time goes in v7:
time: 98.7 us; the launch traced here: 97.6 us
  Pallas kernels  96.3 us (98%)
    pallas_call x1, Pallas kernels, per_device(): pl.pallas_call(kernel, out_shape=pltpu.VMEM((PASSES, 2 * PART), F32), in_...  96.3 us

profile of v7, /device:TPU:6, one launch (start us, length us, event | category | flops | bytes accessed | tf_op | source)
XLA Modules:
  0.0 97.6 jit_solution(15095379157286879953)
XLA Ops:
  0.6 96.3 %passages.1 = f32[24,1024]{1,0:T(8,128)S(1)} custom-call(s32[24]{0:T(128)} %lengths.1, s32[24]{0:T(128)} %assign.1, bf16[384,512]{1,0:T(8,128)(2,1)} %bitcast.3, f32[32,128]{1,0:T(8,128)} %bitcast.4, bf16[128,896]{1,0:T(8,128)(2,1)} %gate.1, bf16[128,896]{1,0:T(8,128)(2,1)} %up.1, bf16[896,128]{1,0:T(8,128)(2,1)} %down.1, f32[1,512]{1,0:T(1,128)} %bitcast.5, ...), custom_call_target="tpu_custom_call" | custom-call | tf_op jit(solution)/shard_map/passages/pallas_call | solution.py:520
  96.9 0.6 slice_subtract_fusion

commit v8 on v7

--- a/solution.py
+++ b/solution.py
@@ -47,7 +47,7 @@
     out,
     wbuf, xbuf, acc, cbuf, dbuf, sbuf, g_in, u_in, gain_in, og_in,
     scale_s, mask_s, inv_s, hb, hb2, hid, tf, tb, r1b, qs, rb, rb7, mine_m, other_m, sb, abuf, pick, cacc, resp, gotc, chosen_s, smean, out_s,
-    ss, rs, ls,
+    ss, rs, ls, word,
 ):
     lst = lax.axis_index("list")
     ten = lax.axis_index("tensor")
@@ -117,19 +117,16 @@
     cp_o = local(out_gain, og_in)
     barrier = pltpu.get_barrier_semaphore()
 
-    def greet_list(i):
-        pl.semaphore_signal(barrier, inc=1, device_id=dev(list_=lax.rem(lst + i, 32)), device_id_type=MESH)
-
-    def greet_x(i):
-        pl.semaphore_signal(barrier, inc=1, device_id=dev(tensor=lax.rem(ten + 2 * i, 8)), device_id_type=MESH)
-
-    def greet_across(i):
-        there = dev(list_=zl * 8 + lax.rem(y + i, 4) * 2 + core, tensor=x * 2 + 1 - zh)
-        pl.semaphore_signal(barrier, inc=1, device_id=there, device_id_type=MESH)
-
-    greet_across(0)
-    pl.loop(1, 4)(greet_x)
-    pl.loop(1, 32)(greet_list)
+    def ring_z(step):
+        z_ = lax.rem(zh * 4 + zl + step + 8, 8)
+        return dev(list_=lax.rem(z_, 4) * 8 + me_g, tensor=x * 2 + z_ // 4)
+
+    def greet(semaphore, devices):
+        for there in devices:
+            pl.semaphore_signal(semaphore, inc=1, device_id=there, device_id_type=MESH)
+
+    near = [at_x(2), at_y(2), ring_z(1), ring_z(-1), at_y(1), at_y(-1), at_x(1), at_x(-1), sibling]
+    greet(barrier, near)
     for cp in cps_w:
         cp.wait()
     eye = lax.broadcasted_iota(jnp.int32, (128, 128), 0) == lax.broadcasted_iota(jnp.int32, (128, 128), 1)
@@ -139,7 +136,7 @@
         wbuf[own_rows, j * 256 : j * 256 + 128] = (g_in[:, j * 128 : j * 128 + 128].astype(F32) * gcol).astype(BF)
         wbuf[own_rows, j * 256 + 128 : j * 256 + 256] = (u_in[:, j * 128 : j * 128 + 128].astype(F32) * gcol).astype(BF)
 
-    pl.semaphore_wait(barrier, 31 + 3 + 1)
+    pl.semaphore_wait(barrier, len(near))
     for step in (1, -1, 2):
         for half in range(2):
             send(states.at[:, pl.ds(half * 256, 256)], xslot(zh, half, x), S_X, R_X + half, at_x(step))
@@ -259,6 +256,12 @@
         acol = jnp.where(sub == p, assign[p], acol)
         lcol = jnp.where(sub == p, lengths[p], lcol)
     abuf[lst] = arow
+
+    greet(word.at[0], [sibling])
+    pl.semaphore_wait(word.at[0], 1)
+    for r in range(1, 5):
+        greet(word.at[r], [ring_z(1), ring_z(-1)])
+        pl.semaphore_wait(word.at[r], 2)
 
     @pl.loop(1, 32)
     def _(i):
@@ -559,6 +562,7 @@
             pltpu.SemaphoreType.DMA((S_END,)),
             pltpu.SemaphoreType.DMA((R_END,)),
             pltpu.SemaphoreType.DMA((10,)),
+            pltpu.SemaphoreType.REGULAR((5,)),
         ],
         compiler_params=pltpu.CompilerParams(collective_id=0, has_side_effects=True, vmem_limit_bytes=56 << 20),
         name="passages",

time: 98.7 us -> 96.6 us (0.979)
  Pallas kernels: 96.3 us -> 93.7 us
    pallas_call x1, Pallas kernels: 96.3 us -> 93.7 us  [per_device(): pl.pallas_call(kernel, out_shape=pltpu.VMEM((PASSES, 2 * PART), F32), in_...]
where the time goes in v8:
time: 96.6 us; the launch traced here: 95 us
  Pallas kernels  93.7 us (97%)
    pallas_call x1, Pallas kernels, per_device(): pl.pallas_call(kernel, out_shape=pltpu.VMEM((PASSES, 2 * PART), F32), in_...  93.7 us

profile of v8, /device:TPU:6, one launch (start us, length us, event | category | flops | bytes accessed | tf_op | source)
XLA Modules:
  0.0 95.0 jit_solution(15830002545984241555)
XLA Ops:
  0.6 93.7 %passages.1 = f32[24,1024]{1,0:T(8,128)S(1)} custom-call(s32[24]{0:T(128)} %lengths.1, s32[24]{0:T(128)} %assign.1, bf16[384,512]{1,0:T(8,128)(2,1)} %bitcast.3, f32[32,128]{1,0:T(8,128)} %bitcast.4, bf16[128,896]{1,0:T(8,128)(2,1)} %gate.1, bf16[128,896]{1,0:T(8,128)(2,1)} %up.1, bf16[896,128]{1,0:T(8,128)(2,1)} %down.1, f32[1,512]{1,0:T(1,128)} %bitcast.5, ...), custom_call_target="tpu_custom_call" | custom-call | tf_op jit(solution)/shard_map/passages/pallas_call | solution.py:523
  94.3 0.6 slice_subtract_fusion

commit v9 on v8

--- a/solution.py
+++ b/solution.py
@@ -125,7 +125,7 @@
         for there in devices:
             pl.semaphore_signal(semaphore, inc=1, device_id=there, device_id_type=MESH)
 
-    near = [at_x(2), at_y(2), ring_z(1), ring_z(-1), at_y(1), at_y(-1), at_x(1), at_x(-1), sibling]
+    near = [ring_z(1), ring_z(-1), at_y(1), at_y(-1), at_x(1), at_x(-1), sibling]
     greet(barrier, near)
     for cp in cps_w:
         cp.wait()
@@ -137,9 +137,12 @@
         wbuf[own_rows, j * 256 + 128 : j * 256 + 256] = (u_in[:, j * 128 : j * 128 + 128].astype(F32) * gcol).astype(BF)
 
     pl.semaphore_wait(barrier, len(near))
-    for step in (1, -1, 2):
+    def x_send(step):
         for half in range(2):
             send(states.at[:, pl.ds(half * 256, 256)], xslot(zh, half, x), S_X, R_X + half, at_x(step))
+
+    x_send(1)
+    x_send(-1)
 
     def piece(z_hi, n, p, x_):
         rows = pl.ds(0, ROWS) if n == 0 else pl.ds(p * (ROWS // 2), ROWS // 2)
@@ -257,11 +260,11 @@
         lcol = jnp.where(sub == p, lengths[p], lcol)
     abuf[lst] = arow
 
-    greet(word.at[0], [sibling])
-    pl.semaphore_wait(word.at[0], 1)
-    for r in range(1, 5):
-        greet(word.at[r], [ring_z(1), ring_z(-1)])
-        pl.semaphore_wait(word.at[r], 2)
+    for r in range(5):
+        greet(word.at[r], near)
+        pl.semaphore_wait(word.at[r], len(near))
+        if r == 0:
+            x_send(2)
 
     @pl.loop(1, 32)
     def _(i):
@@ -349,9 +352,6 @@
         down_to(zl, near_end)
 
     crossed(1, 0)
-    halves(1)
-    from_sibling_neighbours(2)
-    product(y_a, 2)
     x_arrived(2)
     for k in range(4):
         from_sibling_column(k)
@@ -362,6 +362,9 @@
         down_from(3 - zl)
         down_to(3 - zl, near_end)
 
+    halves(1)
+    from_sibling_neighbours(2)
+    product(y_a, 2)
     squares_of((1 - zh) * 2 + lax.rem(y, 2), False)
     halves(2)
     for k in range(2):

time: 96.6 us -> 96 us (level); the launches traced: 95 us -> 95.7 us
  no operation moved by 1% of the time
where the time goes in v9:
time: 96 us; the launch traced here: 95.7 us
  Pallas kernels  94.4 us (98%)
    pallas_call x1, Pallas kernels, per_device(): pl.pallas_call(kernel, out_shape=pltpu.VMEM((PASSES, 2 * PART), F32), in_...  94.4 us

profile of v9, /device:TPU:6, one launch (start us, length us, event | category | flops | bytes accessed | tf_op | source)
XLA Modules:
  0.0 95.7 jit_solution(1116196586861602315)
XLA Ops:
  0.6 94.4 %passages.1 = f32[24,1024]{1,0:T(8,128)S(1)} custom-call(s32[24]{0:T(128)} %lengths.1, s32[24]{0:T(128)} %assign.1, bf16[384,512]{1,0:T(8,128)(2,1)} %bitcast.3, f32[32,128]{1,0:T(8,128)} %bitcast.4, bf16[128,896]{1,0:T(8,128)(2,1)} %gate.1, bf16[128,896]{1,0:T(8,128)(2,1)} %up.1, bf16[896,128]{1,0:T(8,128)(2,1)} %down.1, f32[1,512]{1,0:T(1,128)} %bitcast.5, ...), custom_call_target="tpu_custom_call" | custom-call | tf_op jit(solution)/shard_map/passages/pallas_call | solution.py:526
  95.0 0.6 slice_subtract_fusion

commit v10 on v9

--- a/solution.py
+++ b/solution.py
@@ -109,24 +109,24 @@
     def xslot(z_hi, half, x_):
         return xbuf.at[z_hi * 2 + half, :, pl.ds(pl.multiple_of(x_ * 256, 256), 256)]
 
+    barrier = pltpu.get_barrier_semaphore()
+
+    def ring_z(step):
+        z_ = lax.rem(zh * 4 + zl + step + 8, 8)
+        return dev(list_=lax.rem(z_, 4) * 8 + me_g, tensor=x * 2 + z_ // 4)
+
+    def greet(semaphore, devices):
+        for there in devices:
+            pl.semaphore_signal(semaphore, inc=1, device_id=there, device_id_type=MESH)
+
+    near = [ring_z(1), ring_z(-1), at_y(1), at_y(-1), at_x(1), at_x(-1), sibling]
+    greet(barrier, near)
     cps_w = [local(gate, g_in), local(up, u_in), local(gain, gain_in)]
     cps_x = [local(states.at[:, pl.ds(half * 256, 256)], xslot(zh, half, x)) for half in range(2)]
     cp_d = local(down, dslot(zl, core))
     cp_s = local(states, sbuf)
     cp_c = local(centroids, cbuf)
     cp_o = local(out_gain, og_in)
-    barrier = pltpu.get_barrier_semaphore()
-
-    def ring_z(step):
-        z_ = lax.rem(zh * 4 + zl + step + 8, 8)
-        return dev(list_=lax.rem(z_, 4) * 8 + me_g, tensor=x * 2 + z_ // 4)
-
-    def greet(semaphore, devices):
-        for there in devices:
-            pl.semaphore_signal(semaphore, inc=1, device_id=there, device_id_type=MESH)
-
-    near = [ring_z(1), ring_z(-1), at_y(1), at_y(-1), at_x(1), at_x(-1), sibling]
-    greet(barrier, near)
     for cp in cps_w:
         cp.wait()
     eye = lax.broadcasted_iota(jnp.int32, (128, 128), 0) == lax.broadcasted_iota(jnp.int32, (128, 128), 1)
@@ -341,8 +341,8 @@
     cp_d.wait()
     down_to(zl, jnp.where(inner_z, 3 - zl, near_mid))
     down_over(zl)
+    neighbour(2)
     cross(1, 0)
-    neighbour(2)
     pl.when(outer_z)(lambda: column(3))
     cross(1, 1)
     @pl.when(inner_z)

time: 96 us -> 96.1 us (level)
  no operation moved by 1% of the time
where the time goes in v10:
time: 96.1 us; the launch traced here: 95.8 us
  Pallas kernels  94.5 us (98%)
    pallas_call x1, Pallas kernels, per_device(): pl.pallas_call(kernel, out_shape=pltpu.VMEM((PASSES, 2 * PART), F32), in_...  94.5 us

profile of v10, /device:TPU:6, one launch (start us, length us, event | category | flops | bytes accessed | tf_op | source)
XLA Modules:
  0.0 95.8 jit_solution(12762832860606504726)
XLA Ops:
  0.6 94.5 %passages.1 = f32[24,1024]{1,0:T(8,128)S(1)} custom-call(s32[24]{0:T(128)} %lengths.1, s32[24]{0:T(128)} %assign.1, bf16[384,512]{1,0:T(8,128)(2,1)} %bitcast.3, f32[32,128]{1,0:T(8,128)} %bitcast.4, bf16[128,896]{1,0:T(8,128)(2,1)} %gate.1, bf16[128,896]{1,0:T(8,128)(2,1)} %up.1, bf16[896,128]{1,0:T(8,128)(2,1)} %down.1, f32[1,512]{1,0:T(1,128)} %bitcast.5, ...), custom_call_target="tpu_custom_call" | custom-call | tf_op jit(solution)/shard_map/passages/pallas_call | solution.py:526
  95.1 0.6 slice_subtract_fusion
